TPU v7x, 256 devices: a whole 4x4x8 slice. The times are simulated.
256 devices in a mesh: block: 16 (over x, z_hi, core), day: 16 (over y, z_lo).
Axes of the slice: x: 4, y: 4, z: 8 (z_hi: 2, z_lo: 4; z = z_hi * 4 + z_lo), core: 2. Of those that a mesh axis runs over, the one named last changes fastest.
Arguments:
- spectra: bfloat16 [16, 8, 256, 2, 4096], P('day', None, 'block'), may hold values from -6 to 6
- hour_mask: int32 [16, 8, 256], P('day', None, 'block'), may hold values 0 or 1
- pairs: int32 [16, 2], replicated, may hold values from 0 to 15, as said below
Outputs:
- correlation: float32 [16, 256, 2048], P('block', 'day')
Inputs may be any that keep to these rules, and one draw needn't show every extreme that they name: `pairs`: rows k * 8 to (k + 1) * 8 - 1 form round k: every block appears in exactly one of its rows, so the two entries of a row differ.
All inputs are finite; a program needn't handle non-finite values. No bound on the sum of `hour_mask` on one device may be relied on, other than what follows from the above.
Results may differ from a plain program's by a relative error of at most 0.004.
Values may be sent and summed in bfloat16 or wider, within the bound.
No kernel may reach another device: no remote copies, remote signals or barrier semaphores. Data moves between devices by JAX's collectives and lax.ppermute only.
A program may use at most 128 MiB of HBM per device.

v0:
```python
import math

import jax
import jax.numpy as jnp
from jax import lax
from jax.sharding import PartitionSpec as P

F = 4096
LAGS = 2048


def tables(first, count, lags, width):
    bins = first + jnp.arange(count, dtype=jnp.int32)
    shifts = jnp.arange(lags, dtype=jnp.int32) - lags // 2
    turns = jnp.mod((bins + 1)[:, None] * shifts[None, :], 2 * width)
    phase = turns.astype(jnp.float32) * (math.pi / width)
    return (jnp.cos(phase), jnp.sin(phase))


def cross_terms(left, right):
    left_re = left[:, :, :, None, 0].astype(jnp.float32)
    left_im = left[:, :, :, None, 1].astype(jnp.float32)
    right_re = right[:, :, None, :, 0].astype(jnp.float32)
    right_im = right[:, :, None, :, 1].astype(jnp.float32)
    cross_re = jnp.sum(left_re * right_re + left_im * right_im, axis=0)
    cross_im = jnp.sum(left_im * right_re - left_re * right_im, axis=0)
    return (cross_re, cross_im)


def shards(spectra, hour_mask, pairs):
    blocks_count = lax.axis_size("block")
    days_count = lax.axis_size("day") * spectra.shape[0]
    stations = spectra.shape[2]
    values = spectra[0].astype(jnp.float32)
    power = jnp.mean(values[:, :, 0] * values[:, :, 0] + values[:, :, 1] * values[:, :, 1], axis=-1)
    factor = hour_mask[0].astype(jnp.float32) / jnp.sqrt(power + 1e-06)
    whitened = (values * factor[:, :, None, None]).astype(jnp.bfloat16)
    spread = lax.all_to_all(whitened, "block", split_axis=3, concat_axis=1, tiled=True)
    hours = spread.shape[0]
    band_part = spread.shape[3]
    grouped = spread.reshape(hours, blocks_count, stations, 2, band_part)
    left = jnp.take(grouped, pairs[:, 0], axis=1)
    right = jnp.take(grouped, pairs[:, 1], axis=1)
    cross_re, cross_im = cross_terms(left, right)
    pair_count = cross_re.shape[0]
    cross_re = cross_re.reshape(pair_count, stations * stations, band_part)
    cross_im = cross_im.reshape(pair_count, stations * stations, band_part)
    scale = 1.0 / math.sqrt(F * hours * days_count)
    high = lax.Precision.HIGHEST
    summed_re, summed_im = (
        lax.psum_scatter(cross_re, "day", scatter_dimension=1, tiled=True),
        lax.psum_scatter(cross_im, "day", scatter_dimension=1, tiled=True),
    )
    row_count = summed_re.shape[1]
    offset = lax.axis_index("block") * band_part
    cos_table, sin_table = tables(offset, band_part, LAGS, F)
    flat_re = summed_re.reshape(-1, band_part)
    flat_im = summed_im.reshape(-1, band_part)
    lagged = jnp.dot(flat_re, cos_table, precision=high) - jnp.dot(
        flat_im, sin_table, precision=high
    )
    result = lax.psum_scatter(lagged * scale, "block", scatter_dimension=0, tiled=True)
    return result.reshape(pair_count // blocks_count, row_count, LAGS)


def solution(mesh):
    in_specs = (P("day", None, "block", None, None), P("day", None, "block"), P())
    out_specs = P("block", "day", None)
    return jax.shard_map(shards, mesh=mesh, in_specs=in_specs, out_specs=out_specs, check_vma=False)
```

profile of v0, /device:TPU:1, one launch (start us, length us, event | category | flops | bytes accessed | tf_op | source)
XLA Modules:
  0.0 523.8 jit_solution(7528432776630027660)
XLA Ops:
  6.5 21.7 %copy.32 = bf16[1,8,16,2,4096]{2,1,3,4,0:T(8,128)(2,1)} copy(bf16[1,8,16,2,4096]{4,3,2,1,0:T(2,128)(2,1)} %param.5) | data formatting | bytes 4194304 | tf_op args[0]
  28.2 21.6 %bitcast_convert_fusion = f32[8,16,2,4096]{1,0,2,3:T(8,128)} fusion(bf16[1,8,16,2,4096]{2,1,3,4,0:T(8,128)(2,1)} %copy.32), kind=kLoop, calls=%fused_computation.9 | loop fusion | flops 1048576 | bytes 6291456 | tf_op jit(solution)/shard_map/convert_element_type | solution.py:34
  49.8 12.1 %fusion.1 = f32[8,16]{1,0:T(8,128)S(1)} fusion(f32[8,16,2,4096]{1,0,2,3:T(8,128)} %bitcast_convert_fusion), kind=kLoop, calls=%fused_computation.7 | loop fusion | flops 2097024 | bytes 4194816 | tf_op jit(solution)/shard_map/reduce_sum | solution.py:35
  61.9 0.0 copy-done
  61.9 0.0 slice-done
  61.9 0.0 slice-done.1
  61.9 0.0 slice-done.2
  61.9 0.0 slice-done.3
  62.0 7.6 %fusion.23 = bf16[4096,2,8,16]{3,2,1,0:T(8,128)(2,1)} fusion(f32[8,16]{1,0:T(8,128)S(1)} %bitcast_multiply_fusion, bf16[1,8,16,2,4096]{2,1,3,4,0:T(8,128)(2,1)S(1)} %bitcast.52), kind=kLoop, calls=%fused_computation.50 | loop fusion | flops 3145728 | bytes 4194816
  69.6 20.8 %reshape.98 = bf16[16,2,32768]{2,1,0:T(2,128)(2,1)} reshape(bf16[4096,2,8,16]{3,2,1,0:T(8,128)(2,1)} %fusion.23) | data formatting | bytes 4194304
  90.4 12.6 %all-to-all-start = ((bf16[16,2,32768]{2,1,0:T(2,128)(2,1)}), bf16[16,2,32768]{2,1,0:T(2,128)(2,1)S(1)}, u32[]{:S(2)}, u32[]{:S(2)}) async-start(bf16[16,2,32768]{2,1,0:T(2,128)(2,1)} %reshape.98), calls=%async_computation | async-start | bytes 4194304 | tf_op jit(solution)/shard_map/all_to_all | solution.py:38
  102.9 0.0 reduce-scatter.4.cloned.1.call-start
  103.0 0.0 copy-done.1
  103.0 37.2 %all-to-all-done = bf16[16,2,32768]{2,1,0:T(2,128)(2,1)S(1)} async-done(((bf16[16,2,32768]{2,1,0:T(2,128)(2,1)}), bf16[16,2,32768]{2,1,0:T(2,128)(2,1)S(1)}, u32[]{:S(2)}, u32[]{:S(2)}) %all-to-all-start) | async-done | bytes 2097184 | tf_op jit(solution)/shard_map/all_to_all | solution.py:38
  140.2 14.3 %reshape.99 = bf16[4096,2,8,16]{3,2,1,0:T(8,128)(2,1)} reshape(bf16[16,2,32768]{2,1,0:T(2,128)(2,1)S(1)} %all-to-all-done) | data formatting | bytes 4194304
  154.5 17.1 %copy.34 = bf16[8,16,2,16,256]{4,1,2,3,0:T(8,128)(2,1)S(1)} copy(bf16[8,16,2,16,256]{1,0,2,4,3:T(8,128)(2,1)} %bitcast.53) | data formatting | bytes 4194304 | tf_op jit(solution)/shard_map/all_to_all | solution.py:38
  171.6 2.0 gather_fusion
  173.6 2.0 gather_fusion.1
  175.6 2.6 select_bitcast_fusion
  178.2 0.6 fusion.12
  178.9 1.7 fusion.11
  180.6 23.3 %subtract_reduce_fusion = (f32[16,16,16,256]{3,2,1,0:T(8,128)}, f32[16,16,16,256]{3,2,1,0:T(8,128)}) fusion(f32[8,16,16,256]{3,2,0,1:T(8,128)S(1)} %get-tuple-element.12, f32[8,16,16,256]{3,2,0,1:T(8,128)S(1)} %get-tuple-element.14, f32[8,16,16,256]{3,2,0,1:T(8,128)S(1)} %get-tuple-element.13, f32[8,16,16,256]{3,2,0,1:T(8,128)} %get-tuple-element.15), kind=kLoop, calls=%fused_computation.2 | loop fusion | flops 65011712 | bytes 16777216 | tf_op jit(solution)/shard_map/reduce_sum | solution.py:26
  203.9 0.0 reduce-scatter.4.cloned.1.call-update
  203.9 0.0 reduce-scatter.6.cloned.1.call-start
  204.0 0.7 reduce-scatter.6.cloned.1.call-update
  204.7 0.2 reduce-scatter.8.cloned.1.call-start
  205.0 110.9 %reduce-scatter.4.cloned.1.call-done = f32[16,16,256]{2,1,0:T(8,128)} async-done(((f32[16,256,256]{2,1,0:T(8,128)}), f32[16,16,256]{2,1,0:T(8,128)}) %reduce-scatter.4.cloned.1.call-update) | async-done | bytes 262160 | tf_op jit(solution)/shard_map/reduce_scatter | solution.py:51
  315.8 10.4 %fusion.7 = f32[256,2048]{1,0:T(8,128)S(1)} fusion(f32[256,256]{1,0:T(8,128)} %bitcast.58, s32[2048]{0:T(1024)S(1)} %iota_add_fusion, s32[256]{0:T(256)S(1)} %add_add_fusion), kind=kOutput, calls=%fused_computation.23 | convolution fusion | flops 1617952768 | bytes 2368512 | tf_op jit(solution)/shard_map/dot_general | solution.py:59
  326.3 92.4 %reduce-scatter.6.cloned.1.call-done = f32[16,16,256]{2,1,0:T(8,128)} async-done(((f32[16,256,256]{2,1,0:T(8,128)}), f32[16,16,256]{2,1,0:T(8,128)}) %reduce-scatter.6.cloned.1.call-update) | async-done | bytes 262160 | tf_op jit(solution)/shard_map/reduce_scatter | solution.py:52
  418.7 11.9 %fusion.2 = f32[256,2048]{1,0:T(8,128)} fusion(f32[256,2048]{1,0:T(8,128)S(1)} %fusion.7, f32[256,256]{1,0:T(8,128)} %bitcast.59, s32[2048]{0:T(1024)S(1)} %iota_add_fusion, s32[256]{0:T(256)S(1)} %add_add_fusion), kind=kOutput, calls=%fused_computation.16 | convolution fusion | flops 1619001344 | bytes 4465664 | tf_op jit(solution)/shard_map/dot_general | solution.py:59
  430.6 0.0 reduce-scatter.8.cloned.1.call-update
  430.6 86.7 %reduce-scatter.8.cloned.1.call-done = f32[16,2048]{1,0:T(8,128)} async-done(((f32[256,2048]{1,0:T(8,128)}), f32[16,2048]{1,0:T(8,128)}) %reduce-scatter.8.cloned.1.call-update) | async-done | bytes 131088 | tf_op jit(solution)/shard_map/reduce_scatter | solution.py:62
  (13 shorter events, 0.0 us)
Async XLA Ops:
  28.2 33.7 %slice-start = ((s8[16777216]{0:T(1024)(128)(4,1)}), s8[4194304]{0:T(1024)(128)(4,1)S(1)}, s32[]{:S(2)}) async-start(s8[16777216]{0:T(1024)(128)(4,1)} %bitcast.51), calls=%async_computation.7 | async-start | bytes 8388608
  28.2 33.7 %slice-start.1 = ((s8[16777216]{0:T(1024)(128)(4,1)}), s8[4194304]{0:T(1024)(128)(4,1)S(1)}, s32[]{:S(2)}) async-start(s8[16777216]{0:T(1024)(128)(4,1)} %bitcast.51), calls=%async_computation.8 | async-start | bytes 8388608
  28.2 33.7 %slice-start.2 = ((s8[16777216]{0:T(1024)(128)(4,1)}), s8[4194304]{0:T(1024)(128)(4,1)S(1)}, s32[]{:S(2)}) async-start(s8[16777216]{0:T(1024)(128)(4,1)} %bitcast.51), calls=%async_computation.9 | async-start | bytes 8388608
  49.8 12.1 %copy-start = (s32[1,8,16]{2,1,0:T(8,128)S(1)}, s32[1,8,16]{2,1,0:T(8,128)}, u32[]{:S(2)}) copy-start(s32[1,8,16]{2,1,0:T(8,128)} %param.6) | copy-start | bytes 1540
  49.8 12.1 %slice-start.3 = ((s8[16777216]{0:T(1024)(128)(4,1)}), s8[4194304]{0:T(1024)(128)(4,1)S(1)}, s32[]{:S(2)}) async-start(s8[16777216]{0:T(1024)(128)(4,1)} %bitcast.51), calls=%async_computation.10 | async-start | bytes 8388608
  90.4 12.6 %copy-start.1 = (s32[16,2]{0,1:T(2,128)S(1)}, s32[16,2]{0,1:T(2,128)}, u32[]{:S(2)}) copy-start(s32[16,2]{0,1:T(2,128)} %param.7) | copy-start | bytes 388
  90.4 49.8 %all-to-all-start = ((bf16[16,2,32768]{2,1,0:T(2,128)(2,1)}), bf16[16,2,32768]{2,1,0:T(2,128)(2,1)S(1)}, u32[]{:S(2)}, u32[]{:S(2)}) async-start(bf16[16,2,32768]{2,1,0:T(2,128)(2,1)} %reshape.98), calls=%async_computation | async-start | bytes 4194304 | tf_op jit(solution)/shard_map/all_to_all | solution.py:38
  102.9 212.9 %reduce-scatter.4.cloned.1.call-start = ((), (), s32[]{:S(2)}) async-start(), calls=%async_computation.4 | async-start | bytes 4456448 | tf_op jit(solution)/shard_map/reduce_scatter | solution.py:51
  203.9 214.7 %reduce-scatter.6.cloned.1.call-start = ((), (), s32[]{:S(2)}) async-start(), calls=%async_computation.5 | async-start | bytes 4456448 | tf_op jit(solution)/shard_map/reduce_scatter | solution.py:52
  204.7 312.6 %reduce-scatter.8.cloned.1.call-start = ((), (), s32[]{:S(2)}) async-start(), calls=%async_computation.6 | async-start | bytes 2228224 | tf_op jit(solution)/shard_map/reduce_scatter | solution.py:62
Sparse Core Ops, SparseCore 0:
  204.1 111.7 reduce-scatter.3
  318.4 100.2 reduce-scatter.5
  430.7 86.4 reduce-scatter.7
where the time goes:
time: 525 us; the launch traced here: 524 us
  waiting for transfers between devices  328 us (62%)
  local copies, waits for them, and re-layouts  77.8 us (15%)
  other arithmetic  69.7 us (13%)
  matrix products  22.4 us (4%)
  between operations  13.3 us (3%)
  starting transfers between devices  12.9 us (2%)
    reduce_scatter x1, waiting for transfers between devices, shards(): lax.psum_scatter(cross_re, 'day', scatter_dimension=1, tiled=True)  111 us
    reduce_scatter x1, waiting for transfers between devices, shards(): lax.psum_scatter(cross_im, 'day', scatter_dimension=1, tiled=True)  92.4 us
    reduce_scatter x1, waiting for transfers between devices, shards(): lax.psum_scatter(lagged * scale, 'block', scatter_dimension=0, tiled=True)  86.7 us
    unnamed x15, local copies, waits for them, and re-layouts  56.7 us
    all_to_all x1, waiting for transfers between devices, shards(): lax.all_to_all(whitened, 'block', split_axis=3, concat_axis=1, tiled=True)  37.2 us
    reduce_sum x1, other arithmetic, cross_terms(): cross_im = jnp.sum(left_im * right_re - left_re * right_im, axis=0)  23.3 us
    convert_element_type x1, other arithmetic, shards(): values = spectra[0].astype(jnp.float32)  21.6 us
    all_to_all x1, local copies, waits for them, and re-layouts, shards(): lax.all_to_all(whitened, 'block', split_axis=3, concat_axis=1, tiled=True)  17.1 us
  transfers between devices with their start and end apart: 4, of which 4 were waited for; matrix products, arithmetic and copies ran while one was open for 2% of the time, Pallas kernels for 0%

commit v1 on v0

v1 whole, which is shorter than its diff:
```python
import functools
import math

import jax
import jax.numpy as jnp
from jax import lax
from jax.experimental import pallas as pl
from jax.experimental.pallas import tpu as pltpu
from jax.sharding import PartitionSpec as P

F = 4096
LAGS = 2048
S_BLK = 16
HOURS = 8
DAYS = 16
BLOCKS = 16
PAIRS = 16
LANES = 128
TILES = F // LANES
GROUPS = 8
BINS = 16
DEVICES = 256
COARSE = 512
BOTH = ("block", "day")
VMEM = pl.BlockSpec(memory_space=pltpu.VMEM)
SMEM = pl.BlockSpec(memory_space=pltpu.SMEM)


def lane_index(shape):
    return lax.broadcasted_iota(jnp.int32, shape, len(shape) - 1)


def barrel(vectors, position):
    count = len(vectors)
    step = 1
    while step < count:
        mask = (position & step) != 0
        vectors = [jnp.where(mask, vectors[(n + step) % count], vectors[n]) for n in range(count)]
        step *= 2
    return vectors


def whiten_kernel(x_ref, mask_ref, out_ref, rows_ref, factor_ref):
    eye = lax.broadcasted_iota(jnp.int32, (S_BLK, S_BLK), 0) == lane_index((S_BLK, S_BLK))

    def hour(h, carry):
        for s in range(S_BLK):
            start = pl.multiple_of(h * (S_BLK * 64) + s * 64, 64)
            values = x_ref[pl.ds(start, 64), :].astype(jnp.float32)
            rows_ref[h, pl.ds(s, 64, stride=S_BLK), :] = values
        total = jnp.zeros((S_BLK, LANES), jnp.float32)
        for part in range(64):
            wide = rows_ref[h, part * S_BLK : (part + 1) * S_BLK, :]
            total = total + wide * wide
        power = jnp.sum(total, axis=1, keepdims=True) * (1.0 / F)
        valid = jnp.broadcast_to(mask_ref[pl.ds(h, 1), :].astype(jnp.float32), (S_BLK, S_BLK))
        valid = jnp.sum(jnp.where(eye, valid, 0.0), axis=1, keepdims=True)
        factor = valid / jnp.sqrt(power + 1e-06)
        factor_ref[h] = jnp.broadcast_to(factor, (S_BLK, LANES))
        return carry

    lax.fori_loop(0, HOURS, hour, 0)
    position = lane_index((S_BLK, LANES)) // BINS

    def part(tc, carry):
        start = pl.multiple_of(tc * S_BLK, S_BLK)
        rolled = []
        for h in range(HOURS):
            value = rows_ref[h, pl.ds(start, S_BLK), :] * factor_ref[h]
            rolled.append(pltpu.roll(value, BINS * h, 1) if h else value)
        mixed = barrel(rolled, position)
        tile = tc // 2
        side = tc % 2
        for g in range(GROUPS):
            row = pl.multiple_of((tile * GROUPS + g) * (2 * S_BLK) + side * S_BLK, S_BLK)
            out_ref[pl.ds(row, S_BLK), :] = mixed[(-g) % GROUPS].astype(jnp.bfloat16)
        return carry

    lax.fori_loop(0, 2 * TILES, part, 0)


def cross_kernel(pairs_ref, x_ref, out_ref, whole_ref, left_ref, keep_ref, flat_ref):
    position = lane_index((S_BLK, LANES)) % BINS

    def block(b, carry):
        for c in range(2):
            rolled = []
            for d in range(DAYS):
                row = pl.multiple_of((b * DAYS + d) * (2 * S_BLK) + c * S_BLK, S_BLK)
                value = x_ref[pl.ds(row, S_BLK), :].astype(jnp.float32)
                rolled.append(pltpu.roll(value, d, 1) if d else value)
            mixed = barrel(rolled, position)
            row = pl.multiple_of(b * S_BLK, S_BLK)
            for u in range(BINS):
                whole_ref[u, pl.ds(row, S_BLK), c * LANES : (c + 1) * LANES] = mixed[
                    (-u) % BINS
                ].astype(jnp.bfloat16)
        return carry

    lax.fori_loop(0, BLOCKS, block, 0)
    owner = lane_index((S_BLK, 256)) // S_BLK
    for p in range(PAIRS):
        keep_ref[p * S_BLK : (p + 1) * S_BLK, :] = (owner == pairs_ref[p, 1]).astype(jnp.float32)
    from_j = lax.broadcasted_iota(jnp.int32, (256, LANES), 0) % S_BLK
    to_lane = lane_index((256, LANES))

    def tile(t, carry):
        total = jnp.zeros((256, LANES), jnp.float32)
        for uu in range(4):
            u = t * 4 + uu
            for p in range(PAIRS):
                first = pl.multiple_of(pairs_ref[p, 0] * S_BLK, S_BLK)
                re = whole_ref[u, pl.ds(first, S_BLK), 0:LANES]
                im = whole_ref[u, pl.ds(first, S_BLK), LANES : 2 * LANES]
                here = slice(p * S_BLK, (p + 1) * S_BLK)
                there = slice(256 + p * S_BLK, 256 + (p + 1) * S_BLK)
                left_ref[here, 0:LANES] = re
                left_ref[here, LANES : 2 * LANES] = im
                left_ref[there, 0:LANES] = im
                left_ref[there, LANES : 2 * LANES] = -re
            for c in range(2):
                gram = lax.dot_general(
                    left_ref[c * 256 : (c + 1) * 256, :],
                    whole_ref[u],
                    (((1,), (1,)), ((), ())),
                    preferred_element_type=jnp.float32,
                )
                kept = (gram * keep_ref[...]).astype(jnp.bfloat16)
                place = (to_lane == from_j + (uu * 2 + c) * S_BLK).astype(jnp.bfloat16)
                total = total + jnp.dot(kept, place, preferred_element_type=jnp.float32)
        flat_ref[pl.ds(t, 256, stride=4), :] = total
        return carry

    lax.fori_loop(0, 4, tile, 0)
    out_ref[...] = flat_ref[...].astype(jnp.bfloat16)


def lag_kernel(x_ref, high_ref, low_ref, cos_ref, sin_ref, out_ref, flat_ref):
    flat_ref[...] = x_ref[...].astype(jnp.float32)
    sums = [jnp.zeros((S_BLK, COARSE), jnp.float32) for _ in range(4)]
    for t in range(4):
        part = flat_ref[pl.ds(t, 256, stride=4), :].T.astype(jnp.bfloat16)
        both = jnp.dot(part, high_ref[...], preferred_element_type=jnp.float32) + jnp.dot(
            part, low_ref[...], preferred_element_type=jnp.float32
        )
        for uu in range(4):
            re = both[uu * 32 : uu * 32 + 16]
            im = both[uu * 32 + 16 : uu * 32 + 32]
            sum_re = re[:, :COARSE] - im[:, COARSE:]
            sum_im = re[:, COARSE:] + im[:, :COARSE]
            for w in range(4):
                row = (t * 4 + uu) * 4 + w
                sums[w] = sums[w] + (
                    sum_re * cos_ref[row : row + 1, :] - sum_im * sin_ref[row : row + 1, :]
                )
    for w in range(4):
        out_ref[:, w * COARSE : (w + 1) * COARSE] = sums[w]


def coarse_tables():
    turns = jnp.arange(256, dtype=jnp.int32)[:, None] * jnp.arange(COARSE, dtype=jnp.int32)[None, :]
    phase = jnp.mod(turns, COARSE).astype(jnp.float32) * (2 * math.pi / COARSE)
    table = jnp.concatenate([jnp.cos(phase), jnp.sin(phase)], axis=1)
    high = lax.reduce_precision(table, 8, 7)
    return high.astype(jnp.bfloat16), (table - high).astype(jnp.bfloat16)


def fine_tables(scale):
    shift = (
        jnp.arange(4, dtype=jnp.int32)[:, None] * COARSE
        + jnp.arange(COARSE, dtype=jnp.int32)[None, :]
        - LAGS // 2
    )
    turns = (jnp.arange(BINS, dtype=jnp.int32) + 1)[:, None, None] * shift[None]
    phase = jnp.mod(turns, 2 * F).astype(jnp.float32) * (math.pi / F)
    phase = phase.reshape(BINS * 4, COARSE)
    return jnp.cos(phase) * scale, jnp.sin(phase) * scale


def shards(spectra, hour_mask, pairs):
    values = spectra.reshape(HOURS, S_BLK, 2, TILES, LANES).transpose(0, 1, 3, 2, 4)
    values = values.reshape(HOURS * S_BLK * TILES * 2, LANES)
    whitened = pl.pallas_call(
        whiten_kernel,
        out_shape=jax.ShapeDtypeStruct((DEVICES * 2 * S_BLK, LANES), jnp.bfloat16),
        in_specs=[VMEM, VMEM],
        out_specs=VMEM,
        scratch_shapes=[
            pltpu.VMEM((HOURS, 64 * S_BLK, LANES), jnp.float32),
            pltpu.VMEM((HOURS, S_BLK, LANES), jnp.float32),
        ],
        compiler_params=pltpu.CompilerParams(vmem_limit_bytes=40 * 1024 * 1024),
        name="whiten",
    )(values, hour_mask[0])
    spread = lax.all_to_all(
        whitened.reshape(DEVICES, 2 * S_BLK, LANES), BOTH, split_axis=0, concat_axis=0, tiled=True
    )
    cross = pl.pallas_call(
        cross_kernel,
        out_shape=jax.ShapeDtypeStruct((DEVICES * 4, LANES), jnp.bfloat16),
        in_specs=[SMEM, VMEM],
        out_specs=VMEM,
        scratch_shapes=[
            pltpu.VMEM((BINS, 256, 256), jnp.bfloat16),
            pltpu.VMEM((512, 256), jnp.bfloat16),
            pltpu.VMEM((256, 256), jnp.float32),
            pltpu.VMEM((DEVICES * 4, LANES), jnp.float32),
        ],
        compiler_params=pltpu.CompilerParams(vmem_limit_bytes=40 * 1024 * 1024),
        name="cross",
    )(pairs, spread.reshape(DEVICES * 2 * S_BLK, LANES))
    owned = lax.all_to_all(
        cross.reshape(DEVICES, 4, LANES), BOTH, split_axis=0, concat_axis=0, tiled=True
    )
    high, low = coarse_tables()
    cos_fine, sin_fine = fine_tables(1.0 / math.sqrt(F * HOURS * DAYS))
    result = pl.pallas_call(
        lag_kernel,
        out_shape=jax.ShapeDtypeStruct((S_BLK, LAGS), jnp.float32),
        in_specs=[VMEM] * 5,
        out_specs=VMEM,
        scratch_shapes=[pltpu.VMEM((DEVICES * 4, LANES), jnp.float32)],
        compiler_params=pltpu.CompilerParams(vmem_limit_bytes=40 * 1024 * 1024),
        name="lag",
    )(owned.reshape(DEVICES * 4, LANES), high, low, cos_fine, sin_fine)
    return result.reshape(1, S_BLK, LAGS)


def solution(mesh):
    in_specs = (P("day", None, "block", None, None), P("day", None, "block"), P())
    out_specs = P("block", "day", None)
    return jax.shard_map(shards, mesh=mesh, in_specs=in_specs, out_specs=out_specs, check_vma=False)
```

time: 525 us -> 113 us (0.22)
  waiting for transfers between devices: 328 us -> 66.2 us
  local copies, waits for them, and re-layouts: 77.8 us -> 2.59 us
  other arithmetic: 69.7 us -> 2.92 us
  matrix products: 22.4 us -> 0 us
  Pallas kernels: 0 us -> 19.6 us
  between operations: 13.3 us -> 0.08 us
  starting transfers between devices: 12.9 us -> 21.2 us
    reduce_scatter x3 -> x0, waiting for transfers between devices: 290 us -> none  [the longest x1 111 us: shards(): lax.psum_scatter(cross_re, 'day', scatter_dimension=1, tiled=True)]
    unnamed x15 -> x7, local copies, waits for them, and re-layouts: 56.7 us -> 2.36 us
    reduce_sum x2 -> x0, other arithmetic: 35.4 us -> none  [the longest x1 23.3 us: cross_terms(): cross_im = jnp.sum(left_im * right_re - left_re * right_im, axis=0)]
    all_to_all x1 -> x2, waiting for transfers between devices: 37.2 us -> 66.2 us  [the longest x1 53.6 us: shards(): lax.all_to_all(whitened.reshape(DEVICES, 2 * S_BLK, LANES), BOTH, split_a...]
    convert_element_type x2 -> x1, other arithmetic: 23.3 us -> 0.19 us  [coarse_tables(): return (high.astype(jnp.bfloat16), (table - high).astype(jnp.bfloat16))]
    dot_general x2 -> x0, matrix products: 22.4 us -> none  [the longest x1 11.9 us: shards(): jnp.dot(flat_im, sin_table, precision=high)]
    pallas_call x0 -> x3, Pallas kernels: none -> 19.6 us  [the longest x1 10.4 us: shards(): pl.pallas_call(whiten_kernel, out_shape=jax.ShapeDtypeStruct((DEVICES * 2...]
    all_to_all x1 -> x0, local copies, waits for them, and re-layouts: 17.1 us -> none  [shards(): lax.all_to_all(whitened, 'block', split_axis=3, concat_axis=1, tiled=True)]
  transfers between devices with their start and end apart: 4 -> 2, of which waited for: 4 -> 2; matrix products, arithmetic and copies ran while one was open for 2% -> 3% of each run, Pallas kernels for 0% -> 0%
where the time goes in v1:
time: 113 us
  waiting for transfers between devices  66.2 us (59%)
  starting transfers between devices  21.2 us (19%)
  Pallas kernels  19.6 us (17%)
  other arithmetic  2.92 us (3%)
  local copies, waits for them, and re-layouts  2.59 us (2%)
    all_to_all x1, waiting for transfers between devices, shards(): lax.all_to_all(whitened.reshape(DEVICES, 2 * S_BLK, LANES), BOTH, split_a...  53.6 us
    all_to_all x1, starting transfers between devices, shards(): lax.all_to_all(whitened.reshape(DEVICES, 2 * S_BLK, LANES), BOTH, split_a...  15.7 us
    all_to_all x1, waiting for transfers between devices, shards(): lax.all_to_all(cross.reshape(DEVICES, 4, LANES), BOTH, split_axis=0, conc...  12.6 us
    pallas_call x1, Pallas kernels, shards(): pl.pallas_call(whiten_kernel, out_shape=jax.ShapeDtypeStruct((DEVICES * 2...  10.4 us
    pallas_call x1, Pallas kernels, shards(): pl.pallas_call(cross_kernel, out_shape=jax.ShapeDtypeStruct((DEVICES * 4,...  7.62 us
    all_to_all x1, starting transfers between devices, shards(): lax.all_to_all(cross.reshape(DEVICES, 4, LANES), BOTH, split_axis=0, conc...  5.57 us
    unnamed x7, local copies, waits for them, and re-layouts  2.36 us
  transfers between devices with their start and end apart: 2, of which 2 were waited for; matrix products, arithmetic and copies ran while one was open for 3% of the time, Pallas kernels for 0%

profile of v1, /device:TPU:1, one launch (start us, length us, event | category | flops | bytes accessed | tf_op | source)
XLA Modules:
  0.0 112.7 jit_solution(4866760209365356653)
XLA Ops:
  0.0 0.0 copy-start
  0.0 1.6 %copy-done = bf16[1,8,16,2,4096]{4,3,2,1,0:T(2,128)(2,1)S(1)} copy-done((bf16[1,8,16,2,4096]{4,3,2,1,0:T(2,128)(2,1)S(1)}, bf16[1,8,16,2,4096]{4,3,2,1,0:T(2,128)(2,1)}, u32[]{:S(2)}) %copy-start) | copy-done | bytes 2097176
  1.6 0.0 copy-start.1
  1.6 0.7 copy-done.1
  2.3 10.4 %whiten.1 = bf16[8192,128]{1,0:T(8,128)(2,1)} custom-call(bf16[8192,128]{1,0:T(8,128)(2,1)S(1)} %bitcast.12, s32[8,16]{1,0:T(8,128)S(1)} %bitcast.14), custom_call_target="tpu_custom_call" | custom-call | tf_op jit(solution)/shard_map/whiten/pallas_call | solution.py:183
  12.7 0.0 copy-start.2
  12.7 15.7 %all-to-all-start = ((bf16[256,32,128]{2,1,0:T(8,128)(2,1)}), bf16[256,32,128]{2,1,0:T(8,128)(2,1)S(1)}, u32[]{:S(2)}, u32[]{:S(2)}) async-start(bf16[256,32,128]{2,1,0:T(8,128)(2,1)} %bitcast.4), calls=%async_computation | async-start | bytes 4194304 | tf_op jit(solution)/shard_map/all_to_all | solution.py:195
  28.4 0.0 copy-done.2
  28.4 0.1 copy.7.pairs_ref
  28.4 0.1 add_add_fusion
  28.5 53.6 %all-to-all-done = bf16[256,32,128]{2,1,0:T(8,128)(2,1)S(1)} async-done(((bf16[256,32,128]{2,1,0:T(8,128)(2,1)}), bf16[256,32,128]{2,1,0:T(8,128)(2,1)S(1)}, u32[]{:S(2)}, u32[]{:S(2)}) %all-to-all-start) | async-done | bytes 2097184 | tf_op jit(solution)/shard_map/all_to_all | solution.py:195
  82.2 7.6 %cross.1 = bf16[1024,128]{1,0:T(8,128)(2,1)} custom-call(s32[16,2]{1,0:T(8,128)S(1)} %copy.7.pairs_ref, bf16[8192,128]{1,0:T(8,128)(2,1)S(1)} %bitcast.11), custom_call_target="tpu_custom_call" | custom-call | tf_op jit(solution)/shard_map/cross/pallas_call | solution.py:198
  89.8 5.6 %all-to-all-start.1 = ((bf16[256,4,128]{2,1,0:T(4,128)(2,1)}), bf16[256,4,128]{2,1,0:T(4,128)(2,1)S(1)}, u32[]{:S(2)}, u32[]{:S(2)}) async-start(bf16[256,4,128]{2,1,0:T(4,128)(2,1)} %bitcast.6), calls=%async_computation.1 | async-start | bytes 524288 | tf_op jit(solution)/shard_map/all_to_all | solution.py:212
  95.5 0.1 mul.89
  95.5 0.1 mul.90
  95.6 2.1 %fusion.7 = (f32[256,512]{1,0:T(8,128)S(1)}, f32[256,512]{1,0:T(8,128)S(1)}) fusion(), kind=kLoop, calls=%fused_computation.13 | loop fusion | flops 1835008 | bytes 1048576 | tf_op jit(solution)/shard_map/sin | solution.py:163
  97.7 0.2 fusion
  97.9 0.6 sine_multiply_fusion
  98.5 12.6 %all-to-all-done.1 = bf16[256,4,128]{2,1,0:T(4,128)(2,1)S(1)} async-done(((bf16[256,4,128]{2,1,0:T(4,128)(2,1)}), bf16[256,4,128]{2,1,0:T(4,128)(2,1)S(1)}, u32[]{:S(2)}, u32[]{:S(2)}) %all-to-all-start.1) | async-done | bytes 262176 | tf_op jit(solution)/shard_map/all_to_all | solution.py:212
  111.1 1.6 %lag.1 = f32[16,2048]{1,0:T(8,128)} custom-call(bf16[1024,128]{1,0:T(8,128)(2,1)S(1)} %bitcast.13, bf16[256,1024]{1,0:T(8,128)(2,1)S(1)} %get-tuple-element.6.high_ref, bf16[256,1024]{1,0:T(8,128)(2,1)S(1)} %get-tuple-element.5.low_ref, f32[64,512]{1,0:T(8,128)S(1)} %get-tuple-element.8.cos_ref, f32[64,512]{1,0:T(8,128)S(1)} %get-tuple-element.7.sin_ref), custom_call_target="tpu_custom_call" | custom-call | tf_op jit(solution)/shard_map/lag/pallas_call | solution.py:217
  (4 shorter events, 0.1 us)
Async XLA Ops:
  0.0 1.6 %copy-start = (bf16[1,8,16,2,4096]{4,3,2,1,0:T(2,128)(2,1)S(1)}, bf16[1,8,16,2,4096]{4,3,2,1,0:T(2,128)(2,1)}, u32[]{:S(2)}) copy-start(bf16[1,8,16,2,4096]{4,3,2,1,0:T(2,128)(2,1)} %param.3) | copy-start | bytes 6291460
  1.6 0.7 copy-start.1
  12.7 15.7 %copy-start.2 = (s32[16,2]{0,1:T(2,128)S(1)}, s32[16,2]{0,1:T(2,128)}, u32[]{:S(2)}) copy-start(s32[16,2]{0,1:T(2,128)} %param.5) | copy-start | bytes 388
  12.7 69.5 %all-to-all-start = ((bf16[256,32,128]{2,1,0:T(8,128)(2,1)}), bf16[256,32,128]{2,1,0:T(8,128)(2,1)S(1)}, u32[]{:S(2)}, u32[]{:S(2)}) async-start(bf16[256,32,128]{2,1,0:T(8,128)(2,1)} %bitcast.4), calls=%async_computation | async-start | bytes 4194304 | tf_op jit(solution)/shard_map/all_to_all | solution.py:195
  89.8 21.3 %all-to-all-start.1 = ((bf16[256,4,128]{2,1,0:T(4,128)(2,1)}), bf16[256,4,128]{2,1,0:T(4,128)(2,1)S(1)}, u32[]{:S(2)}, u32[]{:S(2)}) async-start(bf16[256,4,128]{2,1,0:T(4,128)(2,1)} %bitcast.6), calls=%async_computation.1 | async-start | bytes 524288 | tf_op jit(solution)/shard_map/all_to_all | solution.py:212

commit v2 on v1

--- a/solution.py
+++ b/solution.py
@@ -1,4 +1,3 @@
-import functools
 import math
 
 import jax
@@ -41,97 +40,87 @@
 
 
 def whiten_kernel(x_ref, mask_ref, out_ref, rows_ref, factor_ref):
-    eye = lax.broadcasted_iota(jnp.int32, (S_BLK, S_BLK), 0) == lane_index((S_BLK, S_BLK))
-
-    def hour(h, carry):
+    step = pl.program_id(0)
+
+    @pl.when(step < HOURS)
+    def _():
         for s in range(S_BLK):
-            start = pl.multiple_of(h * (S_BLK * 64) + s * 64, 64)
-            values = x_ref[pl.ds(start, 64), :].astype(jnp.float32)
-            rows_ref[h, pl.ds(s, 64, stride=S_BLK), :] = values
-        total = jnp.zeros((S_BLK, LANES), jnp.float32)
+            values = x_ref[s * 64 : (s + 1) * 64, :].astype(jnp.float32)
+            rows_ref[step, pl.ds(s, 64, stride=S_BLK), :] = values
+        totals = [jnp.zeros((S_BLK, LANES), jnp.float32) for _ in range(4)]
         for part in range(64):
-            wide = rows_ref[h, part * S_BLK : (part + 1) * S_BLK, :]
-            total = total + wide * wide
+            wide = rows_ref[step, part * S_BLK : (part + 1) * S_BLK, :]
+            totals[part % 4] = totals[part % 4] + wide * wide
+        total = (totals[0] + totals[1]) + (totals[2] + totals[3])
         power = jnp.sum(total, axis=1, keepdims=True) * (1.0 / F)
-        valid = jnp.broadcast_to(mask_ref[pl.ds(h, 1), :].astype(jnp.float32), (S_BLK, S_BLK))
+        eye = lax.broadcasted_iota(jnp.int32, (S_BLK, S_BLK), 0) == lane_index((S_BLK, S_BLK))
+        valid = jnp.broadcast_to(mask_ref[pl.ds(step, 1), :].astype(jnp.float32), (S_BLK, S_BLK))
         valid = jnp.sum(jnp.where(eye, valid, 0.0), axis=1, keepdims=True)
         factor = valid / jnp.sqrt(power + 1e-06)
-        factor_ref[h] = jnp.broadcast_to(factor, (S_BLK, LANES))
+        factor_ref[step] = jnp.broadcast_to(factor, (S_BLK, LANES))
+
+    @pl.when(step >= HOURS)
+    def _():
+        position = lane_index((S_BLK, LANES)) // BINS
+        first = (step - HOURS) * 16
+        for part in range(16):
+            start = pl.multiple_of((first + part) * S_BLK, S_BLK)
+            rolled = []
+            for h in range(HOURS):
+                value = (rows_ref[h, pl.ds(start, S_BLK), :] * factor_ref[h]).astype(jnp.bfloat16)
+                rolled.append(pltpu.roll(value, BINS * h, 1) if h else value)
+            mixed = barrel(rolled, position)
+            for g in range(GROUPS):
+                row = (part // 2 * GROUPS + g) * (2 * S_BLK) + part % 2 * S_BLK
+                out_ref[row : row + S_BLK, :] = mixed[(-g) % GROUPS]
+
+
+def cross_kernel(pairs_ref, x_ref, out_ref, whole_ref, keep_ref, flat_ref):
+    position = lane_index((S_BLK, LANES)) % BINS
+
+    def block(step, carry):
+        for k in range(2):
+            b = step * 2 + k
+            for c in range(2):
+                rolled = []
+                for d in range(DAYS):
+                    row = pl.multiple_of((b * DAYS + d) * (2 * S_BLK) + c * S_BLK, S_BLK)
+                    value = x_ref[pl.ds(row, S_BLK), :]
+                    rolled.append(pltpu.roll(value, d, 1) if d else value)
+                mixed = barrel(rolled, position)
+                row = pl.multiple_of(b * S_BLK, S_BLK)
+                for u in range(BINS):
+                    whole_ref[u, pl.ds(row, S_BLK), c * LANES : (c + 1) * LANES] = mixed[(-u) % BINS]
         return carry
 
-    lax.fori_loop(0, HOURS, hour, 0)
-    position = lane_index((S_BLK, LANES)) // BINS
-
-    def part(tc, carry):
-        start = pl.multiple_of(tc * S_BLK, S_BLK)
-        rolled = []
-        for h in range(HOURS):
-            value = rows_ref[h, pl.ds(start, S_BLK), :] * factor_ref[h]
-            rolled.append(pltpu.roll(value, BINS * h, 1) if h else value)
-        mixed = barrel(rolled, position)
-        tile = tc // 2
-        side = tc % 2
-        for g in range(GROUPS):
-            row = pl.multiple_of((tile * GROUPS + g) * (2 * S_BLK) + side * S_BLK, S_BLK)
-            out_ref[pl.ds(row, S_BLK), :] = mixed[(-g) % GROUPS].astype(jnp.bfloat16)
-        return carry
-
-    lax.fori_loop(0, 2 * TILES, part, 0)
-
-
-def cross_kernel(pairs_ref, x_ref, out_ref, whole_ref, left_ref, keep_ref, flat_ref):
-    position = lane_index((S_BLK, LANES)) % BINS
-
-    def block(b, carry):
-        for c in range(2):
-            rolled = []
-            for d in range(DAYS):
-                row = pl.multiple_of((b * DAYS + d) * (2 * S_BLK) + c * S_BLK, S_BLK)
-                value = x_ref[pl.ds(row, S_BLK), :].astype(jnp.float32)
-                rolled.append(pltpu.roll(value, d, 1) if d else value)
-            mixed = barrel(rolled, position)
-            row = pl.multiple_of(b * S_BLK, S_BLK)
-            for u in range(BINS):
-                whole_ref[u, pl.ds(row, S_BLK), c * LANES : (c + 1) * LANES] = mixed[
-                    (-u) % BINS
-                ].astype(jnp.bfloat16)
-        return carry
-
-    lax.fori_loop(0, BLOCKS, block, 0)
+    lax.fori_loop(0, BLOCKS // 2, block, 0)
     owner = lane_index((S_BLK, 256)) // S_BLK
     for p in range(PAIRS):
         keep_ref[p * S_BLK : (p + 1) * S_BLK, :] = (owner == pairs_ref[p, 1]).astype(jnp.float32)
     from_j = lax.broadcasted_iota(jnp.int32, (256, LANES), 0) % S_BLK
     to_lane = lane_index((256, LANES))
-
-    def tile(t, carry):
+    firsts = [pl.multiple_of(pairs_ref[p, 0] * S_BLK, S_BLK) for p in range(PAIRS)]
+    for t in range(4):
         total = jnp.zeros((256, LANES), jnp.float32)
         for uu in range(4):
             u = t * 4 + uu
-            for p in range(PAIRS):
-                first = pl.multiple_of(pairs_ref[p, 0] * S_BLK, S_BLK)
-                re = whole_ref[u, pl.ds(first, S_BLK), 0:LANES]
-                im = whole_ref[u, pl.ds(first, S_BLK), LANES : 2 * LANES]
-                here = slice(p * S_BLK, (p + 1) * S_BLK)
-                there = slice(256 + p * S_BLK, 256 + (p + 1) * S_BLK)
-                left_ref[here, 0:LANES] = re
-                left_ref[here, LANES : 2 * LANES] = im
-                left_ref[there, 0:LANES] = im
-                left_ref[there, LANES : 2 * LANES] = -re
+            re, im = (
+                jnp.concatenate(
+                    [whole_ref[u, pl.ds(first, S_BLK), c * LANES : (c + 1) * LANES] for first in firsts],
+                    axis=0,
+                )
+                for c in range(2)
+            )
+            right = whole_ref[u]
             for c in range(2):
+                left = jnp.concatenate([im, -re] if c else [re, im], axis=1)
                 gram = lax.dot_general(
-                    left_ref[c * 256 : (c + 1) * 256, :],
-                    whole_ref[u],
-                    (((1,), (1,)), ((), ())),
-                    preferred_element_type=jnp.float32,
+                    left, right, (((1,), (1,)), ((), ())), preferred_element_type=jnp.float32
                 )
                 kept = (gram * keep_ref[...]).astype(jnp.bfloat16)
                 place = (to_lane == from_j + (uu * 2 + c) * S_BLK).astype(jnp.bfloat16)
                 total = total + jnp.dot(kept, place, preferred_element_type=jnp.float32)
         flat_ref[pl.ds(t, 256, stride=4), :] = total
-        return carry
-
-    lax.fori_loop(0, 4, tile, 0)
     out_ref[...] = flat_ref[...].astype(jnp.bfloat16)
 
 
@@ -183,8 +172,12 @@
     whitened = pl.pallas_call(
         whiten_kernel,
         out_shape=jax.ShapeDtypeStruct((DEVICES * 2 * S_BLK, LANES), jnp.bfloat16),
-        in_specs=[VMEM, VMEM],
-        out_specs=VMEM,
+        grid=(HOURS + 4,),
+        in_specs=[
+            pl.BlockSpec((S_BLK * 64, LANES), lambda i: (jnp.minimum(i, HOURS - 1), 0)),
+            pl.BlockSpec((HOURS, S_BLK), lambda i: (0, 0)),
+        ],
+        out_specs=pl.BlockSpec((DEVICES * S_BLK // 2, LANES), lambda i: (jnp.maximum(i - HOURS, 0), 0)),
         scratch_shapes=[
             pltpu.VMEM((HOURS, 64 * S_BLK, LANES), jnp.float32),
             pltpu.VMEM((HOURS, S_BLK, LANES), jnp.float32),
@@ -202,7 +195,6 @@
         out_specs=VMEM,
         scratch_shapes=[
             pltpu.VMEM((BINS, 256, 256), jnp.bfloat16),
-            pltpu.VMEM((512, 256), jnp.bfloat16),
             pltpu.VMEM((256, 256), jnp.float32),
             pltpu.VMEM((DEVICES * 4, LANES), jnp.float32),
         ],

time: 113 us -> 106 us (0.938)
  Pallas kernels: 19.6 us -> 12.7 us
    pallas_call x1, Pallas kernels: 10.4 us -> 5.23 us  [shards(): pl.pallas_call(whiten_kernel, out_shape=jax.ShapeDtypeStruct((DEVICES * 2...]
    pallas_call x1, Pallas kernels: 7.62 us -> 5.83 us  [shards(): pl.pallas_call(cross_kernel, out_shape=jax.ShapeDtypeStruct((DEVICES * 4,...]
where the time goes in v2:
time: 106 us
  waiting for transfers between devices  66.2 us (62%)
  starting transfers between devices  21.2 us (20%)
  Pallas kernels  12.7 us (12%)
  other arithmetic  2.92 us (3%)
  local copies, waits for them, and re-layouts  2.59 us (2%)
    all_to_all x1, waiting for transfers between devices, shards(): lax.all_to_all(whitened.reshape(DEVICES, 2 * S_BLK, LANES), BOTH, split_a...  53.6 us
    all_to_all x1, starting transfers between devices, shards(): lax.all_to_all(whitened.reshape(DEVICES, 2 * S_BLK, LANES), BOTH, split_a...  15.7 us
    all_to_all x1, waiting for transfers between devices, shards(): lax.all_to_all(cross.reshape(DEVICES, 4, LANES), BOTH, split_axis=0, conc...  12.6 us
    pallas_call x1, Pallas kernels, shards(): pl.pallas_call(cross_kernel, out_shape=jax.ShapeDtypeStruct((DEVICES * 4,...  5.83 us
    all_to_all x1, starting transfers between devices, shards(): lax.all_to_all(cross.reshape(DEVICES, 4, LANES), BOTH, split_axis=0, conc...  5.58 us
    pallas_call x1, Pallas kernels, shards(): pl.pallas_call(whiten_kernel, out_shape=jax.ShapeDtypeStruct((DEVICES * 2...  5.23 us
    unnamed x7, local copies, waits for them, and re-layouts  2.36 us
  transfers between devices with their start and end apart: 2, of which 2 were waited for; matrix products, arithmetic and copies ran while one was open for 3% of the time, Pallas kernels for 0%

profile of v2, /device:TPU:1, one launch (start us, length us, event | category | flops | bytes accessed | tf_op | source)
XLA Modules:
  0.0 105.7 jit_solution(515163923146527873)
XLA Ops:
  0.0 0.0 copy-start
  0.0 1.6 %copy-done = bf16[1,8,16,2,4096]{4,3,2,1,0:T(2,128)(2,1)S(1)} copy-done((bf16[1,8,16,2,4096]{4,3,2,1,0:T(2,128)(2,1)S(1)}, bf16[1,8,16,2,4096]{4,3,2,1,0:T(2,128)(2,1)}, u32[]{:S(2)}) %copy-start) | copy-done | bytes 2097176
  1.6 0.0 copy-start.1
  1.6 0.7 copy-done.1
  2.3 5.2 %whiten.1 = bf16[8192,128]{1,0:T(8,128)(2,1)} custom-call(bf16[8192,128]{1,0:T(8,128)(2,1)S(1)} %bitcast.12, s32[8,16]{1,0:T(8,128)S(1)} %bitcast.14), custom_call_target="tpu_custom_call" | custom-call | tf_op jit(solution)/shard_map/whiten/pallas_call | solution.py:172
  7.5 0.0 copy-start.2
  7.5 15.7 %all-to-all-start = ((bf16[256,32,128]{2,1,0:T(8,128)(2,1)}), bf16[256,32,128]{2,1,0:T(8,128)(2,1)S(1)}, u32[]{:S(2)}, u32[]{:S(2)}) async-start(bf16[256,32,128]{2,1,0:T(8,128)(2,1)} %bitcast.4), calls=%async_computation | async-start | bytes 4194304 | tf_op jit(solution)/shard_map/all_to_all | solution.py:188
  23.2 0.0 copy-done.2
  23.2 0.1 copy.7.pairs_ref
  23.3 0.1 add_add_fusion
  23.4 53.6 %all-to-all-done = bf16[256,32,128]{2,1,0:T(8,128)(2,1)S(1)} async-done(((bf16[256,32,128]{2,1,0:T(8,128)(2,1)}), bf16[256,32,128]{2,1,0:T(8,128)(2,1)S(1)}, u32[]{:S(2)}, u32[]{:S(2)}) %all-to-all-start) | async-done | bytes 2097184 | tf_op jit(solution)/shard_map/all_to_all | solution.py:188
  77.0 5.8 %cross.1 = bf16[1024,128]{1,0:T(8,128)(2,1)} custom-call(s32[16,2]{1,0:T(8,128)S(1)} %copy.7.pairs_ref, bf16[8192,128]{1,0:T(8,128)(2,1)S(1)} %bitcast.11), custom_call_target="tpu_custom_call" | custom-call | tf_op jit(solution)/shard_map/cross/pallas_call | solution.py:191
  82.8 5.6 %all-to-all-start.1 = ((bf16[256,4,128]{2,1,0:T(4,128)(2,1)}), bf16[256,4,128]{2,1,0:T(4,128)(2,1)S(1)}, u32[]{:S(2)}, u32[]{:S(2)}) async-start(bf16[256,4,128]{2,1,0:T(4,128)(2,1)} %bitcast.6), calls=%async_computation.1 | async-start | bytes 524288 | tf_op jit(solution)/shard_map/all_to_all | solution.py:204
  88.5 0.1 mul.89
  88.6 0.1 mul.90
  88.7 2.1 %fusion.7 = (f32[256,512]{1,0:T(8,128)S(1)}, f32[256,512]{1,0:T(8,128)S(1)}) fusion(), kind=kLoop, calls=%fused_computation.13 | loop fusion | flops 1835008 | bytes 1048576 | tf_op jit(solution)/shard_map/sin | solution.py:152
  90.7 0.2 fusion
  90.9 0.6 sine_multiply_fusion
  91.5 12.6 %all-to-all-done.1 = bf16[256,4,128]{2,1,0:T(4,128)(2,1)S(1)} async-done(((bf16[256,4,128]{2,1,0:T(4,128)(2,1)}), bf16[256,4,128]{2,1,0:T(4,128)(2,1)S(1)}, u32[]{:S(2)}, u32[]{:S(2)}) %all-to-all-start.1) | async-done | bytes 262176 | tf_op jit(solution)/shard_map/all_to_all | solution.py:204
  104.1 1.6 %lag.1 = f32[16,2048]{1,0:T(8,128)} custom-call(bf16[1024,128]{1,0:T(8,128)(2,1)S(1)} %bitcast.13, bf16[256,1024]{1,0:T(8,128)(2,1)S(1)} %get-tuple-element.6.high_ref, bf16[256,1024]{1,0:T(8,128)(2,1)S(1)} %get-tuple-element.5.low_ref, f32[64,512]{1,0:T(8,128)S(1)} %get-tuple-element.8.cos_ref, f32[64,512]{1,0:T(8,128)S(1)} %get-tuple-element.7.sin_ref), custom_call_target="tpu_custom_call" | custom-call | tf_op jit(solution)/shard_map/lag/pallas_call | solution.py:209
  (4 shorter events, 0.1 us)
Async XLA Ops:
  0.0 1.6 %copy-start = (bf16[1,8,16,2,4096]{4,3,2,1,0:T(2,128)(2,1)S(1)}, bf16[1,8,16,2,4096]{4,3,2,1,0:T(2,128)(2,1)}, u32[]{:S(2)}) copy-start(bf16[1,8,16,2,4096]{4,3,2,1,0:T(2,128)(2,1)} %param.3) | copy-start | bytes 6291460
  1.6 0.7 copy-start.1
  7.5 15.7 %copy-start.2 = (s32[16,2]{0,1:T(2,128)S(1)}, s32[16,2]{0,1:T(2,128)}, u32[]{:S(2)}) copy-start(s32[16,2]{0,1:T(2,128)} %param.5) | copy-start | bytes 388
  7.5 69.5 %all-to-all-start = ((bf16[256,32,128]{2,1,0:T(8,128)(2,1)}), bf16[256,32,128]{2,1,0:T(8,128)(2,1)S(1)}, u32[]{:S(2)}, u32[]{:S(2)}) async-start(bf16[256,32,128]{2,1,0:T(8,128)(2,1)} %bitcast.4), calls=%async_computation | async-start | bytes 4194304 | tf_op jit(solution)/shard_map/all_to_all | solution.py:188
  82.8 21.3 %all-to-all-start.1 = ((bf16[256,4,128]{2,1,0:T(4,128)(2,1)}), bf16[256,4,128]{2,1,0:T(4,128)(2,1)S(1)}, u32[]{:S(2)}, u32[]{:S(2)}) async-start(bf16[256,4,128]{2,1,0:T(4,128)(2,1)} %bitcast.6), calls=%async_computation.1 | async-start | bytes 524288 | tf_op jit(solution)/shard_map/all_to_all | solution.py:204

commit v3 on v2

--- a/solution.py
+++ b/solution.py
@@ -20,8 +20,11 @@
 BINS = 16
 DEVICES = 256
 COARSE = 512
+ROWS = 24
+QUARTER = DEVICES * 2 * S_BLK // 4
 BOTH = ("block", "day")
 VMEM = pl.BlockSpec(memory_space=pltpu.VMEM)
+ANY = pl.BlockSpec(memory_space=pl.ANY)
 SMEM = pl.BlockSpec(memory_space=pltpu.SMEM)
 
 
@@ -39,69 +42,87 @@
     return vectors
 
 
-def whiten_kernel(x_ref, mask_ref, out_ref, rows_ref, factor_ref):
-    step = pl.program_id(0)
-
-    @pl.when(step < HOURS)
-    def _():
+def whiten_kernel(
+    x_hbm, mask_hbm, out_hbm, x_ref, mask_ref, rows_ref, factor_ref, out_ref, in_sem, mask_sem, out_sem
+):
+    def read(h):
+        here = x_hbm.at[pl.ds(h * S_BLK * 64, S_BLK * 64)]
+        return pltpu.make_async_copy(here, x_ref.at[h], in_sem.at[h])
+
+    def write(q):
+        here = pl.ds(q * QUARTER, QUARTER)
+        return pltpu.make_async_copy(out_ref.at[here], out_hbm.at[here], out_sem.at[q])
+
+    for h in range(HOURS):
+        read(h).start()
+    mask_copy = pltpu.make_async_copy(mask_hbm, mask_ref, mask_sem)
+    mask_copy.start()
+    mask_copy.wait()
+    eye = lax.broadcasted_iota(jnp.int32, (S_BLK, S_BLK), 0) == lane_index((S_BLK, S_BLK))
+    for h in range(HOURS):
+        read(h).wait()
         for s in range(S_BLK):
-            values = x_ref[s * 64 : (s + 1) * 64, :].astype(jnp.float32)
-            rows_ref[step, pl.ds(s, 64, stride=S_BLK), :] = values
+            values = x_ref[h, s * 64 : (s + 1) * 64, :]
+            if h:
+                values = pltpu.roll(values, BINS * h, 1)
+            rows_ref[h, pl.ds(s, 64, stride=ROWS), :] = values.astype(jnp.float32)
         totals = [jnp.zeros((S_BLK, LANES), jnp.float32) for _ in range(4)]
         for part in range(64):
-            wide = rows_ref[step, part * S_BLK : (part + 1) * S_BLK, :]
+            wide = rows_ref[h, part * ROWS : part * ROWS + S_BLK, :]
             totals[part % 4] = totals[part % 4] + wide * wide
         total = (totals[0] + totals[1]) + (totals[2] + totals[3])
         power = jnp.sum(total, axis=1, keepdims=True) * (1.0 / F)
-        eye = lax.broadcasted_iota(jnp.int32, (S_BLK, S_BLK), 0) == lane_index((S_BLK, S_BLK))
-        valid = jnp.broadcast_to(mask_ref[pl.ds(step, 1), :].astype(jnp.float32), (S_BLK, S_BLK))
+        valid = jnp.broadcast_to(mask_ref[h : h + 1, :].astype(jnp.float32), (S_BLK, S_BLK))
         valid = jnp.sum(jnp.where(eye, valid, 0.0), axis=1, keepdims=True)
-        factor = valid / jnp.sqrt(power + 1e-06)
-        factor_ref[step] = jnp.broadcast_to(factor, (S_BLK, LANES))
-
-    @pl.when(step >= HOURS)
-    def _():
-        position = lane_index((S_BLK, LANES)) // BINS
-        first = (step - HOURS) * 16
+        factor_ref[h] = jnp.broadcast_to(valid / jnp.sqrt(power + 1e-06), (S_BLK, LANES))
+    position = lane_index((S_BLK, LANES)) // BINS
+
+    def quarter(q, carry):
         for part in range(16):
-            start = pl.multiple_of((first + part) * S_BLK, S_BLK)
-            rolled = []
-            for h in range(HOURS):
-                value = (rows_ref[h, pl.ds(start, S_BLK), :] * factor_ref[h]).astype(jnp.bfloat16)
-                rolled.append(pltpu.roll(value, BINS * h, 1) if h else value)
+            start = pl.multiple_of((q * 16 + part) * ROWS, 8)
+            rolled = [
+                (rows_ref[h, pl.ds(start, S_BLK), :] * factor_ref[h]).astype(jnp.bfloat16)
+                for h in range(HOURS)
+            ]
             mixed = barrel(rolled, position)
             for g in range(GROUPS):
                 row = (part // 2 * GROUPS + g) * (2 * S_BLK) + part % 2 * S_BLK
-                out_ref[row : row + S_BLK, :] = mixed[(-g) % GROUPS]
-
-
-def cross_kernel(pairs_ref, x_ref, out_ref, whole_ref, keep_ref, flat_ref):
+                row = pl.multiple_of(q * QUARTER + row, S_BLK)
+                out_ref[pl.ds(row, S_BLK), :] = mixed[(-g) % GROUPS]
+        write(q).start()
+        return carry
+
+    lax.fori_loop(0, 4, quarter, 0)
+    for q in range(4):
+        write(q).wait()
+
+
+def cross_kernel(pairs_ref, x_ref, out_ref, whole_ref, keep_ref, place_ref, flat_ref):
     position = lane_index((S_BLK, LANES)) % BINS
-
-    def block(step, carry):
-        for k in range(2):
-            b = step * 2 + k
-            for c in range(2):
-                rolled = []
-                for d in range(DAYS):
-                    row = pl.multiple_of((b * DAYS + d) * (2 * S_BLK) + c * S_BLK, S_BLK)
-                    value = x_ref[pl.ds(row, S_BLK), :]
-                    rolled.append(pltpu.roll(value, d, 1) if d else value)
-                mixed = barrel(rolled, position)
-                row = pl.multiple_of(b * S_BLK, S_BLK)
-                for u in range(BINS):
-                    whole_ref[u, pl.ds(row, S_BLK), c * LANES : (c + 1) * LANES] = mixed[(-u) % BINS]
-        return carry
-
-    lax.fori_loop(0, BLOCKS // 2, block, 0)
+    for b in range(BLOCKS):
+        for c in range(2):
+            rolled = []
+            for d in range(DAYS):
+                row = (b * DAYS + d) * (2 * S_BLK) + c * S_BLK
+                value = x_ref[row : row + S_BLK, :]
+                rolled.append(pltpu.roll(value, d, 1) if d else value)
+            mixed = barrel(rolled, position)
+            for u in range(BINS):
+                whole_ref[u, b * S_BLK : (b + 1) * S_BLK, c * LANES : (c + 1) * LANES] = mixed[
+                    (-u) % BINS
+                ]
     owner = lane_index((S_BLK, 256)) // S_BLK
     for p in range(PAIRS):
-        keep_ref[p * S_BLK : (p + 1) * S_BLK, :] = (owner == pairs_ref[p, 1]).astype(jnp.float32)
-    from_j = lax.broadcasted_iota(jnp.int32, (256, LANES), 0) % S_BLK
-    to_lane = lane_index((256, LANES))
+        kept = (owner == pairs_ref[p, 1]).astype(jnp.float32)
+        keep_ref[p * S_BLK : (p + 1) * S_BLK, :] = kept.astype(jnp.bfloat16)
+    from_j = lax.broadcasted_iota(jnp.int32, (LANES, LANES), 0) % S_BLK
+    to_lane = lane_index((LANES, LANES))
+    for n in range(8):
+        placed = (to_lane == from_j + n * S_BLK).astype(jnp.float32)
+        place_ref[n * LANES : (n + 1) * LANES, :] = placed.astype(jnp.bfloat16)
     firsts = [pl.multiple_of(pairs_ref[p, 0] * S_BLK, S_BLK) for p in range(PAIRS)]
     for t in range(4):
-        total = jnp.zeros((256, LANES), jnp.float32)
+        folded = []
         for uu in range(4):
             u = t * 4 + uu
             re, im = (
@@ -117,10 +138,11 @@
                 gram = lax.dot_general(
                     left, right, (((1,), (1,)), ((), ())), preferred_element_type=jnp.float32
                 )
-                kept = (gram * keep_ref[...]).astype(jnp.bfloat16)
-                place = (to_lane == from_j + (uu * 2 + c) * S_BLK).astype(jnp.bfloat16)
-                total = total + jnp.dot(kept, place, preferred_element_type=jnp.float32)
-        flat_ref[pl.ds(t, 256, stride=4), :] = total
+                kept = gram.astype(jnp.bfloat16) * keep_ref[...]
+                folded.append(kept[:, :LANES] + kept[:, LANES:])
+        flat_ref[pl.ds(t, 256, stride=4), :] = jnp.dot(
+            jnp.concatenate(folded, axis=1), place_ref[...], preferred_element_type=jnp.float32
+        )
     out_ref[...] = flat_ref[...].astype(jnp.bfloat16)
 
 
@@ -172,17 +194,19 @@
     whitened = pl.pallas_call(
         whiten_kernel,
         out_shape=jax.ShapeDtypeStruct((DEVICES * 2 * S_BLK, LANES), jnp.bfloat16),
-        grid=(HOURS + 4,),
-        in_specs=[
-            pl.BlockSpec((S_BLK * 64, LANES), lambda i: (jnp.minimum(i, HOURS - 1), 0)),
-            pl.BlockSpec((HOURS, S_BLK), lambda i: (0, 0)),
+        in_specs=[ANY, ANY],
+        out_specs=ANY,
+        scratch_shapes=[
+            pltpu.VMEM((HOURS, S_BLK * 64, LANES), jnp.bfloat16),
+            pltpu.VMEM((HOURS, S_BLK), jnp.int32),
+            pltpu.VMEM((HOURS, 64 * ROWS, LANES), jnp.float32),
+            pltpu.VMEM((HOURS, S_BLK, LANES), jnp.float32),
+            pltpu.VMEM((DEVICES * 2 * S_BLK, LANES), jnp.bfloat16),
+            pltpu.SemaphoreType.DMA((HOURS,)),
+            pltpu.SemaphoreType.DMA,
+            pltpu.SemaphoreType.DMA((4,)),
         ],
-        out_specs=pl.BlockSpec((DEVICES * S_BLK // 2, LANES), lambda i: (jnp.maximum(i - HOURS, 0), 0)),
-        scratch_shapes=[
-            pltpu.VMEM((HOURS, 64 * S_BLK, LANES), jnp.float32),
-            pltpu.VMEM((HOURS, S_BLK, LANES), jnp.float32),
-        ],
-        compiler_params=pltpu.CompilerParams(vmem_limit_bytes=40 * 1024 * 1024),
+        compiler_params=pltpu.CompilerParams(vmem_limit_bytes=60 * 1024 * 1024),
         name="whiten",
     )(values, hour_mask[0])
     spread = lax.all_to_all(
@@ -195,7 +219,8 @@
         out_specs=VMEM,
         scratch_shapes=[
             pltpu.VMEM((BINS, 256, 256), jnp.bfloat16),
-            pltpu.VMEM((256, 256), jnp.float32),
+            pltpu.VMEM((256, 256), jnp.bfloat16),
+            pltpu.VMEM((8 * LANES, LANES), jnp.bfloat16),
             pltpu.VMEM((DEVICES * 4, LANES), jnp.float32),
         ],
         compiler_params=pltpu.CompilerParams(vmem_limit_bytes=40 * 1024 * 1024),

time: 106 us -> 101 us (0.953)
  Pallas kernels: 12.7 us -> 10.4 us
  local copies, waits for them, and re-layouts: 2.59 us -> 0.31 us
    unnamed x7 -> x3, local copies, waits for them, and re-layouts: 2.36 us -> 0.09 us
    pallas_call x1, Pallas kernels: 5.83 us -> 3.83 us  [shards(): pl.pallas_call(cross_kernel, out_shape=jax.ShapeDtypeStruct((DEVICES * 4,...]
where the time goes in v3:
time: 101 us
  waiting for transfers between devices  66.2 us (66%)
  starting transfers between devices  21.2 us (21%)
  Pallas kernels  10.4 us (10%)
  other arithmetic  2.92 us (3%)
    all_to_all x1, waiting for transfers between devices, shards(): lax.all_to_all(whitened.reshape(DEVICES, 2 * S_BLK, LANES), BOTH, split_a...  53.6 us
    all_to_all x1, starting transfers between devices, shards(): lax.all_to_all(whitened.reshape(DEVICES, 2 * S_BLK, LANES), BOTH, split_a...  15.7 us
    all_to_all x1, waiting for transfers between devices, shards(): lax.all_to_all(cross.reshape(DEVICES, 4, LANES), BOTH, split_axis=0, conc...  12.6 us
    all_to_all x1, starting transfers between devices, shards(): lax.all_to_all(cross.reshape(DEVICES, 4, LANES), BOTH, split_axis=0, conc...  5.58 us
    pallas_call x1, Pallas kernels, shards(): pl.pallas_call(whiten_kernel, out_shape=jax.ShapeDtypeStruct((DEVICES * 2...  4.95 us
    pallas_call x1, Pallas kernels, shards(): pl.pallas_call(cross_kernel, out_shape=jax.ShapeDtypeStruct((DEVICES * 4,...  3.83 us
    sin x1, other arithmetic, coarse_tables(): table = jnp.concatenate([jnp.cos(phase), jnp.sin(phase)], axis=1)  2.05 us
  transfers between devices with their start and end apart: 2, of which 2 were waited for; matrix products, arithmetic and copies ran while one was open for 3% of the time, Pallas kernels for 0%

profile of v3, /device:TPU:1, one launch (start us, length us, event | category | flops | bytes accessed | tf_op | source)
XLA Modules:
  0.0 101.2 jit_solution(12985464433590067362)
XLA Ops:
  0.0 5.0 %whiten.1 = bf16[8192,128]{1,0:T(8,128)(2,1)} custom-call(bf16[8192,128]{1,0:T(8,128)(2,1)} %bitcast.14, s32[8,16]{1,0:T(8,128)} %bitcast.15), custom_call_target="tpu_custom_call" | custom-call | tf_op jit(solution)/shard_map/whiten/pallas_call | solution.py:194
  5.0 0.0 copy-start
  5.0 15.7 %all-to-all-start = ((bf16[256,32,128]{2,1,0:T(8,128)(2,1)}), bf16[256,32,128]{2,1,0:T(8,128)(2,1)S(1)}, u32[]{:S(2)}, u32[]{:S(2)}) async-start(bf16[256,32,128]{2,1,0:T(8,128)(2,1)} %bitcast.13), calls=%async_computation | async-start | bytes 4194304 | tf_op jit(solution)/shard_map/all_to_all | solution.py:212
  20.6 0.0 copy-done
  20.7 0.1 copy.7.pairs_ref
  20.7 0.1 add_add_fusion
  20.8 53.6 %all-to-all-done = bf16[256,32,128]{2,1,0:T(8,128)(2,1)S(1)} async-done(((bf16[256,32,128]{2,1,0:T(8,128)(2,1)}), bf16[256,32,128]{2,1,0:T(8,128)(2,1)S(1)}, u32[]{:S(2)}, u32[]{:S(2)}) %all-to-all-start) | async-done | bytes 2097184 | tf_op jit(solution)/shard_map/all_to_all | solution.py:212
  74.5 3.8 %cross.1 = bf16[1024,128]{1,0:T(8,128)(2,1)} custom-call(s32[16,2]{1,0:T(8,128)S(1)} %copy.7.pairs_ref, bf16[8192,128]{1,0:T(8,128)(2,1)S(1)} %bitcast.11), custom_call_target="tpu_custom_call" | custom-call | tf_op jit(solution)/shard_map/cross/pallas_call | solution.py:215
  78.3 5.6 %all-to-all-start.1 = ((bf16[256,4,128]{2,1,0:T(4,128)(2,1)}), bf16[256,4,128]{2,1,0:T(4,128)(2,1)S(1)}, u32[]{:S(2)}, u32[]{:S(2)}) async-start(bf16[256,4,128]{2,1,0:T(4,128)(2,1)} %bitcast.6), calls=%async_computation.1 | async-start | bytes 524288 | tf_op jit(solution)/shard_map/all_to_all | solution.py:229
  84.0 0.1 mul.89
  84.0 0.1 mul.90
  84.1 2.1 %fusion.7 = (f32[256,512]{1,0:T(8,128)S(1)}, f32[256,512]{1,0:T(8,128)S(1)}) fusion(), kind=kLoop, calls=%fused_computation.13 | loop fusion | flops 1835008 | bytes 1048576 | tf_op jit(solution)/shard_map/sin | solution.py:174
  86.2 0.2 fusion
  86.4 0.6 sine_multiply_fusion
  87.0 12.6 %all-to-all-done.1 = bf16[256,4,128]{2,1,0:T(4,128)(2,1)S(1)} async-done(((bf16[256,4,128]{2,1,0:T(4,128)(2,1)}), bf16[256,4,128]{2,1,0:T(4,128)(2,1)S(1)}, u32[]{:S(2)}, u32[]{:S(2)}) %all-to-all-start.1) | async-done | bytes 262176 | tf_op jit(solution)/shard_map/all_to_all | solution.py:229
  99.6 1.6 %lag.1 = f32[16,2048]{1,0:T(8,128)} custom-call(bf16[1024,128]{1,0:T(8,128)(2,1)S(1)} %bitcast.12, bf16[256,1024]{1,0:T(8,128)(2,1)S(1)} %get-tuple-element.6.high_ref, bf16[256,1024]{1,0:T(8,128)(2,1)S(1)} %get-tuple-element.5.low_ref, f32[64,512]{1,0:T(8,128)S(1)} %get-tuple-element.8.cos_ref, f32[64,512]{1,0:T(8,128)S(1)} %get-tuple-element.7.sin_ref), custom_call_target="tpu_custom_call" | custom-call | tf_op jit(solution)/shard_map/lag/pallas_call | solution.py:234
  (4 shorter events, 0.1 us)
Async XLA Ops:
  5.0 15.7 %copy-start = (s32[16,2]{0,1:T(2,128)S(1)}, s32[16,2]{0,1:T(2,128)}, u32[]{:S(2)}) copy-start(s32[16,2]{0,1:T(2,128)} %param.5) | copy-start | bytes 388
  5.0 69.5 %all-to-all-start = ((bf16[256,32,128]{2,1,0:T(8,128)(2,1)}), bf16[256,32,128]{2,1,0:T(8,128)(2,1)S(1)}, u32[]{:S(2)}, u32[]{:S(2)}) async-start(bf16[256,32,128]{2,1,0:T(8,128)(2,1)} %bitcast.13), calls=%async_computation | async-start | bytes 4194304 | tf_op jit(solution)/shard_map/all_to_all | solution.py:212
  78.3 21.3 %all-to-all-start.1 = ((bf16[256,4,128]{2,1,0:T(4,128)(2,1)}), bf16[256,4,128]{2,1,0:T(4,128)(2,1)S(1)}, u32[]{:S(2)}, u32[]{:S(2)}) async-start(bf16[256,4,128]{2,1,0:T(4,128)(2,1)} %bitcast.6), calls=%async_computation.1 | async-start | bytes 524288 | tf_op jit(solution)/shard_map/all_to_all | solution.py:229

commit v4 on v3

--- a/solution.py
+++ b/solution.py
@@ -43,7 +43,18 @@
 
 
 def whiten_kernel(
-    x_hbm, mask_hbm, out_hbm, x_ref, mask_ref, rows_ref, factor_ref, out_ref, in_sem, mask_sem, out_sem
+    x_hbm,
+    mask_hbm,
+    out_hbm,
+    x_ref,
+    mask_ref,
+    rows_ref,
+    factor_ref,
+    valid_ref,
+    out_ref,
+    in_sem,
+    mask_sem,
+    out_sem,
 ):
     def read(h):
         here = x_hbm.at[pl.ds(h * S_BLK * 64, S_BLK * 64)]
@@ -53,35 +64,43 @@
         here = pl.ds(q * QUARTER, QUARTER)
         return pltpu.make_async_copy(out_ref.at[here], out_hbm.at[here], out_sem.at[q])
 
+    mask_copy = pltpu.make_async_copy(mask_hbm, mask_ref, mask_sem)
+    mask_copy.start()
     for h in range(HOURS):
         read(h).start()
-    mask_copy = pltpu.make_async_copy(mask_hbm, mask_ref, mask_sem)
-    mask_copy.start()
     mask_copy.wait()
     eye = lax.broadcasted_iota(jnp.int32, (S_BLK, S_BLK), 0) == lane_index((S_BLK, S_BLK))
     for h in range(HOURS):
+        valid = jnp.broadcast_to(mask_ref[h : h + 1, :].astype(jnp.float32), (S_BLK, S_BLK))
+        valid = jnp.sum(jnp.where(eye, valid, 0.0), axis=1, keepdims=True)
+        valid_ref[h * S_BLK : (h + 1) * S_BLK, :] = jnp.broadcast_to(valid, (S_BLK, LANES))
+    for h in range(HOURS):
         read(h).wait()
+        totals = []
         for s in range(S_BLK):
             values = x_ref[h, s * 64 : (s + 1) * 64, :]
             if h:
                 values = pltpu.roll(values, BINS * h, 1)
-            rows_ref[h, pl.ds(s, 64, stride=ROWS), :] = values.astype(jnp.float32)
-        totals = [jnp.zeros((S_BLK, LANES), jnp.float32) for _ in range(4)]
-        for part in range(64):
-            wide = rows_ref[h, part * ROWS : part * ROWS + S_BLK, :]
-            totals[part % 4] = totals[part % 4] + wide * wide
-        total = (totals[0] + totals[1]) + (totals[2] + totals[3])
-        power = jnp.sum(total, axis=1, keepdims=True) * (1.0 / F)
-        valid = jnp.broadcast_to(mask_ref[h : h + 1, :].astype(jnp.float32), (S_BLK, S_BLK))
-        valid = jnp.sum(jnp.where(eye, valid, 0.0), axis=1, keepdims=True)
-        factor_ref[h] = jnp.broadcast_to(valid / jnp.sqrt(power + 1e-06), (S_BLK, LANES))
+            wide = values.astype(jnp.float32)
+            rows_ref[h, pl.ds(s, 64, stride=ROWS), :] = wide
+            squares = wide * wide
+            total = squares[0:8]
+            for r in range(1, 8):
+                total = total + squares[r * 8 : (r + 1) * 8]
+            totals.append(jnp.sum(total, axis=0, keepdims=True))
+        factor_ref[h * S_BLK : (h + 1) * S_BLK, :] = jnp.concatenate(totals, axis=0)
+    power = jnp.sum(factor_ref[...], axis=1, keepdims=True) * (1.0 / F)
+    power = jnp.broadcast_to(power, (HOURS * S_BLK, LANES))
+    factor_ref[...] = valid_ref[...] / jnp.sqrt(power + 1e-06)
     position = lane_index((S_BLK, LANES)) // BINS
 
     def quarter(q, carry):
         for part in range(16):
             start = pl.multiple_of((q * 16 + part) * ROWS, 8)
             rolled = [
-                (rows_ref[h, pl.ds(start, S_BLK), :] * factor_ref[h]).astype(jnp.bfloat16)
+                (rows_ref[h, pl.ds(start, S_BLK), :] * factor_ref[h * S_BLK : (h + 1) * S_BLK, :]).astype(
+                    jnp.bfloat16
+                )
                 for h in range(HOURS)
             ]
             mixed = barrel(rolled, position)
@@ -200,7 +219,8 @@
             pltpu.VMEM((HOURS, S_BLK * 64, LANES), jnp.bfloat16),
             pltpu.VMEM((HOURS, S_BLK), jnp.int32),
             pltpu.VMEM((HOURS, 64 * ROWS, LANES), jnp.float32),
-            pltpu.VMEM((HOURS, S_BLK, LANES), jnp.float32),
+            pltpu.VMEM((HOURS * S_BLK, LANES), jnp.float32),
+            pltpu.VMEM((HOURS * S_BLK, LANES), jnp.float32),
             pltpu.VMEM((DEVICES * 2 * S_BLK, LANES), jnp.bfloat16),
             pltpu.SemaphoreType.DMA((HOURS,)),
             pltpu.SemaphoreType.DMA,

time: 101 us -> 101 us (level)
  no operation moved by 1% of the time
where the time goes in v4:
time: 101 us
  waiting for transfers between devices  66.2 us (66%)
  starting transfers between devices  21.2 us (21%)
  Pallas kernels  9.8 us (10%)
  other arithmetic  2.92 us (3%)
    all_to_all x1, waiting for transfers between devices, shards(): lax.all_to_all(whitened.reshape(DEVICES, 2 * S_BLK, LANES), BOTH, split_a...  53.6 us
    all_to_all x1, starting transfers between devices, shards(): lax.all_to_all(whitened.reshape(DEVICES, 2 * S_BLK, LANES), BOTH, split_a...  15.7 us
    all_to_all x1, waiting for transfers between devices, shards(): lax.all_to_all(cross.reshape(DEVICES, 4, LANES), BOTH, split_axis=0, conc...  12.6 us
    all_to_all x1, starting transfers between devices, shards(): lax.all_to_all(cross.reshape(DEVICES, 4, LANES), BOTH, split_axis=0, conc...  5.57 us
    pallas_call x1, Pallas kernels, shards(): pl.pallas_call(whiten_kernel, out_shape=jax.ShapeDtypeStruct((DEVICES * 2...  4.34 us
    pallas_call x1, Pallas kernels, shards(): pl.pallas_call(cross_kernel, out_shape=jax.ShapeDtypeStruct((DEVICES * 4,...  3.83 us
    sin x1, other arithmetic, coarse_tables(): table = jnp.concatenate([jnp.cos(phase), jnp.sin(phase)], axis=1)  2.05 us
  transfers between devices with their start and end apart: 2, of which 2 were waited for; matrix products, arithmetic and copies ran while one was open for 3% of the time, Pallas kernels for 0%

profile of v4, /device:TPU:1, one launch (start us, length us, event | category | flops | bytes accessed | tf_op | source)
XLA Modules:
  0.0 100.6 jit_solution(12657717168568590225)
XLA Ops:
  0.0 4.3 %whiten.1 = bf16[8192,128]{1,0:T(8,128)(2,1)} custom-call(bf16[8192,128]{1,0:T(8,128)(2,1)} %bitcast.14, s32[8,16]{1,0:T(8,128)} %bitcast.15), custom_call_target="tpu_custom_call" | custom-call | tf_op jit(solution)/shard_map/whiten/pallas_call | solution.py:213
  4.3 0.0 copy-start
  4.4 15.7 %all-to-all-start = ((bf16[256,32,128]{2,1,0:T(8,128)(2,1)}), bf16[256,32,128]{2,1,0:T(8,128)(2,1)S(1)}, u32[]{:S(2)}, u32[]{:S(2)}) async-start(bf16[256,32,128]{2,1,0:T(8,128)(2,1)} %bitcast.13), calls=%async_computation | async-start | bytes 4194304 | tf_op jit(solution)/shard_map/all_to_all | solution.py:232
  20.0 0.0 copy-done
  20.0 0.1 copy.7.pairs_ref
  20.1 0.1 add_add_fusion
  20.2 53.6 %all-to-all-done = bf16[256,32,128]{2,1,0:T(8,128)(2,1)S(1)} async-done(((bf16[256,32,128]{2,1,0:T(8,128)(2,1)}), bf16[256,32,128]{2,1,0:T(8,128)(2,1)S(1)}, u32[]{:S(2)}, u32[]{:S(2)}) %all-to-all-start) | async-done | bytes 2097184 | tf_op jit(solution)/shard_map/all_to_all | solution.py:232
  73.9 3.8 %cross.1 = bf16[1024,128]{1,0:T(8,128)(2,1)} custom-call(s32[16,2]{1,0:T(8,128)S(1)} %copy.7.pairs_ref, bf16[8192,128]{1,0:T(8,128)(2,1)S(1)} %bitcast.11), custom_call_target="tpu_custom_call" | custom-call | tf_op jit(solution)/shard_map/cross/pallas_call | solution.py:235
  77.7 5.6 %all-to-all-start.1 = ((bf16[256,4,128]{2,1,0:T(4,128)(2,1)}), bf16[256,4,128]{2,1,0:T(4,128)(2,1)S(1)}, u32[]{:S(2)}, u32[]{:S(2)}) async-start(bf16[256,4,128]{2,1,0:T(4,128)(2,1)} %bitcast.6), calls=%async_computation.1 | async-start | bytes 524288 | tf_op jit(solution)/shard_map/all_to_all | solution.py:249
  83.4 0.1 mul.89
  83.4 0.1 mul.90
  83.5 2.1 %fusion.7 = (f32[256,512]{1,0:T(8,128)S(1)}, f32[256,512]{1,0:T(8,128)S(1)}) fusion(), kind=kLoop, calls=%fused_computation.13 | loop fusion | flops 1835008 | bytes 1048576 | tf_op jit(solution)/shard_map/sin | solution.py:193
  85.6 0.2 fusion
  85.8 0.6 sine_multiply_fusion
  86.4 12.6 %all-to-all-done.1 = bf16[256,4,128]{2,1,0:T(4,128)(2,1)S(1)} async-done(((bf16[256,4,128]{2,1,0:T(4,128)(2,1)}), bf16[256,4,128]{2,1,0:T(4,128)(2,1)S(1)}, u32[]{:S(2)}, u32[]{:S(2)}) %all-to-all-start.1) | async-done | bytes 262176 | tf_op jit(solution)/shard_map/all_to_all | solution.py:249
  98.9 1.6 %lag.1 = f32[16,2048]{1,0:T(8,128)} custom-call(bf16[1024,128]{1,0:T(8,128)(2,1)S(1)} %bitcast.12, bf16[256,1024]{1,0:T(8,128)(2,1)S(1)} %get-tuple-element.6.high_ref, bf16[256,1024]{1,0:T(8,128)(2,1)S(1)} %get-tuple-element.5.low_ref, f32[64,512]{1,0:T(8,128)S(1)} %get-tuple-element.8.cos_ref, f32[64,512]{1,0:T(8,128)S(1)} %get-tuple-element.7.sin_ref), custom_call_target="tpu_custom_call" | custom-call | tf_op jit(solution)/shard_map/lag/pallas_call | solution.py:254
  (4 shorter events, 0.1 us)
Async XLA Ops:
  4.3 15.7 %copy-start = (s32[16,2]{0,1:T(2,128)S(1)}, s32[16,2]{0,1:T(2,128)}, u32[]{:S(2)}) copy-start(s32[16,2]{0,1:T(2,128)} %param.5) | copy-start | bytes 388
  4.4 69.5 %all-to-all-start = ((bf16[256,32,128]{2,1,0:T(8,128)(2,1)}), bf16[256,32,128]{2,1,0:T(8,128)(2,1)S(1)}, u32[]{:S(2)}, u32[]{:S(2)}) async-start(bf16[256,32,128]{2,1,0:T(8,128)(2,1)} %bitcast.13), calls=%async_computation | async-start | bytes 4194304 | tf_op jit(solution)/shard_map/all_to_all | solution.py:232
  77.7 21.3 %all-to-all-start.1 = ((bf16[256,4,128]{2,1,0:T(4,128)(2,1)}), bf16[256,4,128]{2,1,0:T(4,128)(2,1)S(1)}, u32[]{:S(2)}, u32[]{:S(2)}) async-start(bf16[256,4,128]{2,1,0:T(4,128)(2,1)} %bitcast.6), calls=%async_computation.1 | async-start | bytes 524288 | tf_op jit(solution)/shard_map/all_to_all | solution.py:249

commit v5 on v4

--- a/solution.py
+++ b/solution.py
@@ -20,7 +20,7 @@
 BINS = 16
 DEVICES = 256
 COARSE = 512
-ROWS = 24
+PITCH = 72
 QUARTER = DEVICES * 2 * S_BLK // 4
 BOTH = ("block", "day")
 VMEM = pl.BlockSpec(memory_space=pltpu.VMEM)
@@ -78,11 +78,8 @@
         read(h).wait()
         totals = []
         for s in range(S_BLK):
-            values = x_ref[h, s * 64 : (s + 1) * 64, :]
-            if h:
-                values = pltpu.roll(values, BINS * h, 1)
-            wide = values.astype(jnp.float32)
-            rows_ref[h, pl.ds(s, 64, stride=ROWS), :] = wide
+            wide = x_ref[h, s * 64 : (s + 1) * 64, :].astype(jnp.float32)
+            rows_ref[h, s * PITCH : s * PITCH + 64, :] = wide
             squares = wide * wide
             total = squares[0:8]
             for r in range(1, 8):
@@ -96,13 +93,11 @@
 
     def quarter(q, carry):
         for part in range(16):
-            start = pl.multiple_of((q * 16 + part) * ROWS, 8)
-            rolled = [
-                (rows_ref[h, pl.ds(start, S_BLK), :] * factor_ref[h * S_BLK : (h + 1) * S_BLK, :]).astype(
-                    jnp.bfloat16
-                )
-                for h in range(HOURS)
-            ]
+            rolled = []
+            for h in range(HOURS):
+                wide = rows_ref[h, pl.ds(q * 16 + part, S_BLK, stride=PITCH), :]
+                value = (wide * factor_ref[h * S_BLK : (h + 1) * S_BLK, :]).astype(jnp.bfloat16)
+                rolled.append(pltpu.roll(value, BINS * h, 1) if h else value)
             mixed = barrel(rolled, position)
             for g in range(GROUPS):
                 row = (part // 2 * GROUPS + g) * (2 * S_BLK) + part % 2 * S_BLK
@@ -218,7 +213,7 @@
         scratch_shapes=[
             pltpu.VMEM((HOURS, S_BLK * 64, LANES), jnp.bfloat16),
             pltpu.VMEM((HOURS, S_BLK), jnp.int32),
-            pltpu.VMEM((HOURS, 64 * ROWS, LANES), jnp.float32),
+            pltpu.VMEM((HOURS, S_BLK * PITCH, LANES), jnp.float32),
             pltpu.VMEM((HOURS * S_BLK, LANES), jnp.float32),
             pltpu.VMEM((HOURS * S_BLK, LANES), jnp.float32),
             pltpu.VMEM((DEVICES * 2 * S_BLK, LANES), jnp.bfloat16),

time: 101 us -> 100 us (0.990)
  no operation moved by 1% of the time
where the time goes in v5:
time: 100 us
  waiting for transfers between devices  66.2 us (66%)
  starting transfers between devices  21.2 us (21%)
  Pallas kernels  9.42 us (9%)
  other arithmetic  2.92 us (3%)
    all_to_all x1, waiting for transfers between devices, shards(): lax.all_to_all(whitened.reshape(DEVICES, 2 * S_BLK, LANES), BOTH, split_a...  53.6 us
    all_to_all x1, starting transfers between devices, shards(): lax.all_to_all(whitened.reshape(DEVICES, 2 * S_BLK, LANES), BOTH, split_a...  15.7 us
    all_to_all x1, waiting for transfers between devices, shards(): lax.all_to_all(cross.reshape(DEVICES, 4, LANES), BOTH, split_axis=0, conc...  12.6 us
    all_to_all x1, starting transfers between devices, shards(): lax.all_to_all(cross.reshape(DEVICES, 4, LANES), BOTH, split_axis=0, conc...  5.57 us
    pallas_call x1, Pallas kernels, shards(): pl.pallas_call(whiten_kernel, out_shape=jax.ShapeDtypeStruct((DEVICES * 2...  3.96 us
    pallas_call x1, Pallas kernels, shards(): pl.pallas_call(cross_kernel, out_shape=jax.ShapeDtypeStruct((DEVICES * 4,...  3.84 us
    sin x1, other arithmetic, coarse_tables(): table = jnp.concatenate([jnp.cos(phase), jnp.sin(phase)], axis=1)  2.05 us
  transfers between devices with their start and end apart: 2, of which 2 were waited for; matrix products, arithmetic and copies ran while one was open for 3% of the time, Pallas kernels for 0%

profile of v5, /device:TPU:1, one launch (start us, length us, event | category | flops | bytes accessed | tf_op | source)
XLA Modules:
  0.0 100.2 jit_solution(1978738844333883467)
XLA Ops:
  0.0 4.0 %whiten.1 = bf16[8192,128]{1,0:T(8,128)(2,1)} custom-call(bf16[8192,128]{1,0:T(8,128)(2,1)} %bitcast.14, s32[8,16]{1,0:T(8,128)} %bitcast.15), custom_call_target="tpu_custom_call" | custom-call | tf_op jit(solution)/shard_map/whiten/pallas_call | solution.py:208
  4.0 0.0 copy-start
  4.0 15.7 %all-to-all-start = ((bf16[256,32,128]{2,1,0:T(8,128)(2,1)}), bf16[256,32,128]{2,1,0:T(8,128)(2,1)S(1)}, u32[]{:S(2)}, u32[]{:S(2)}) async-start(bf16[256,32,128]{2,1,0:T(8,128)(2,1)} %bitcast.13), calls=%async_computation | async-start | bytes 4194304 | tf_op jit(solution)/shard_map/all_to_all | solution.py:227
  19.7 0.0 copy-done
  19.7 0.1 copy.7.pairs_ref
  19.7 0.1 add_add_fusion
  19.8 53.6 %all-to-all-done = bf16[256,32,128]{2,1,0:T(8,128)(2,1)S(1)} async-done(((bf16[256,32,128]{2,1,0:T(8,128)(2,1)}), bf16[256,32,128]{2,1,0:T(8,128)(2,1)S(1)}, u32[]{:S(2)}, u32[]{:S(2)}) %all-to-all-start) | async-done | bytes 2097184 | tf_op jit(solution)/shard_map/all_to_all | solution.py:227
  73.5 3.8 %cross.1 = bf16[1024,128]{1,0:T(8,128)(2,1)} custom-call(s32[16,2]{1,0:T(8,128)S(1)} %copy.7.pairs_ref, bf16[8192,128]{1,0:T(8,128)(2,1)S(1)} %bitcast.11), custom_call_target="tpu_custom_call" | custom-call | tf_op jit(solution)/shard_map/cross/pallas_call | solution.py:230
  77.3 5.6 %all-to-all-start.1 = ((bf16[256,4,128]{2,1,0:T(4,128)(2,1)}), bf16[256,4,128]{2,1,0:T(4,128)(2,1)S(1)}, u32[]{:S(2)}, u32[]{:S(2)}) async-start(bf16[256,4,128]{2,1,0:T(4,128)(2,1)} %bitcast.6), calls=%async_computation.1 | async-start | bytes 524288 | tf_op jit(solution)/shard_map/all_to_all | solution.py:244
  83.0 0.1 mul.89
  83.1 0.1 mul.90
  83.1 2.1 %fusion.7 = (f32[256,512]{1,0:T(8,128)S(1)}, f32[256,512]{1,0:T(8,128)S(1)}) fusion(), kind=kLoop, calls=%fused_computation.13 | loop fusion | flops 1835008 | bytes 1048576 | tf_op jit(solution)/shard_map/sin | solution.py:188
  85.2 0.2 fusion
  85.4 0.6 sine_multiply_fusion
  86.0 12.6 %all-to-all-done.1 = bf16[256,4,128]{2,1,0:T(4,128)(2,1)S(1)} async-done(((bf16[256,4,128]{2,1,0:T(4,128)(2,1)}), bf16[256,4,128]{2,1,0:T(4,128)(2,1)S(1)}, u32[]{:S(2)}, u32[]{:S(2)}) %all-to-all-start.1) | async-done | bytes 262176 | tf_op jit(solution)/shard_map/all_to_all | solution.py:244
  98.6 1.6 %lag.1 = f32[16,2048]{1,0:T(8,128)} custom-call(bf16[1024,128]{1,0:T(8,128)(2,1)S(1)} %bitcast.12, bf16[256,1024]{1,0:T(8,128)(2,1)S(1)} %get-tuple-element.6.high_ref, bf16[256,1024]{1,0:T(8,128)(2,1)S(1)} %get-tuple-element.5.low_ref, f32[64,512]{1,0:T(8,128)S(1)} %get-tuple-element.8.cos_ref, f32[64,512]{1,0:T(8,128)S(1)} %get-tuple-element.7.sin_ref), custom_call_target="tpu_custom_call" | custom-call | tf_op jit(solution)/shard_map/lag/pallas_call | solution.py:249
  (4 shorter events, 0.1 us)
Async XLA Ops:
  4.0 15.7 %copy-start = (s32[16,2]{0,1:T(2,128)S(1)}, s32[16,2]{0,1:T(2,128)}, u32[]{:S(2)}) copy-start(s32[16,2]{0,1:T(2,128)} %param.5) | copy-start | bytes 388
  4.0 69.5 %all-to-all-start = ((bf16[256,32,128]{2,1,0:T(8,128)(2,1)}), bf16[256,32,128]{2,1,0:T(8,128)(2,1)S(1)}, u32[]{:S(2)}, u32[]{:S(2)}) async-start(bf16[256,32,128]{2,1,0:T(8,128)(2,1)} %bitcast.13), calls=%async_computation | async-start | bytes 4194304 | tf_op jit(solution)/shard_map/all_to_all | solution.py:227
  77.3 21.3 %all-to-all-start.1 = ((bf16[256,4,128]{2,1,0:T(4,128)(2,1)}), bf16[256,4,128]{2,1,0:T(4,128)(2,1)S(1)}, u32[]{:S(2)}, u32[]{:S(2)}) async-start(bf16[256,4,128]{2,1,0:T(4,128)(2,1)} %bitcast.6), calls=%async_computation.1 | async-start | bytes 524288 | tf_op jit(solution)/shard_map/all_to_all | solution.py:244

commit v6 on v5

--- a/solution.py
+++ b/solution.py
@@ -2,6 +2,8 @@
 
 import jax
 import jax.numpy as jnp
+import ml_dtypes
+import numpy as np
 from jax import lax
 from jax.experimental import pallas as pl
 from jax.experimental.pallas import tpu as pltpu
@@ -127,14 +129,14 @@
                 ]
     owner = lane_index((S_BLK, 256)) // S_BLK
     for p in range(PAIRS):
-        kept = (owner == pairs_ref[p, 1]).astype(jnp.float32)
+        kept = (owner == pairs_ref[1, p]).astype(jnp.float32)
         keep_ref[p * S_BLK : (p + 1) * S_BLK, :] = kept.astype(jnp.bfloat16)
     from_j = lax.broadcasted_iota(jnp.int32, (LANES, LANES), 0) % S_BLK
     to_lane = lane_index((LANES, LANES))
     for n in range(8):
         placed = (to_lane == from_j + n * S_BLK).astype(jnp.float32)
         place_ref[n * LANES : (n + 1) * LANES, :] = placed.astype(jnp.bfloat16)
-    firsts = [pl.multiple_of(pairs_ref[p, 0] * S_BLK, S_BLK) for p in range(PAIRS)]
+    firsts = [pl.multiple_of(pairs_ref[0, p] * S_BLK, S_BLK) for p in range(PAIRS)]
     for t in range(4):
         folded = []
         for uu in range(4):
@@ -183,23 +185,18 @@
 
 
 def coarse_tables():
-    turns = jnp.arange(256, dtype=jnp.int32)[:, None] * jnp.arange(COARSE, dtype=jnp.int32)[None, :]
-    phase = jnp.mod(turns, COARSE).astype(jnp.float32) * (2 * math.pi / COARSE)
-    table = jnp.concatenate([jnp.cos(phase), jnp.sin(phase)], axis=1)
-    high = lax.reduce_precision(table, 8, 7)
-    return high.astype(jnp.bfloat16), (table - high).astype(jnp.bfloat16)
+    turns = np.arange(256)[:, None] * np.arange(COARSE)[None, :] % COARSE
+    phase = turns * (2 * math.pi / COARSE)
+    table = np.concatenate([np.cos(phase), np.sin(phase)], axis=1).astype(np.float32)
+    high = table.astype(ml_dtypes.bfloat16)
+    return high, (table - high.astype(np.float32)).astype(ml_dtypes.bfloat16)
 
 
 def fine_tables(scale):
-    shift = (
-        jnp.arange(4, dtype=jnp.int32)[:, None] * COARSE
-        + jnp.arange(COARSE, dtype=jnp.int32)[None, :]
-        - LAGS // 2
-    )
-    turns = (jnp.arange(BINS, dtype=jnp.int32) + 1)[:, None, None] * shift[None]
-    phase = jnp.mod(turns, 2 * F).astype(jnp.float32) * (math.pi / F)
-    phase = phase.reshape(BINS * 4, COARSE)
-    return jnp.cos(phase) * scale, jnp.sin(phase) * scale
+    shift = np.arange(4)[:, None] * COARSE + np.arange(COARSE)[None, :] - LAGS // 2
+    turns = (np.arange(BINS) + 1)[:, None, None] * shift[None] % (2 * F)
+    phase = (turns * (math.pi / F)).reshape(BINS * 4, COARSE)
+    return (np.cos(phase) * scale).astype(np.float32), (np.sin(phase) * scale).astype(np.float32)
 
 
 def shards(spectra, hour_mask, pairs):
@@ -240,7 +237,7 @@
         ],
         compiler_params=pltpu.CompilerParams(vmem_limit_bytes=40 * 1024 * 1024),
         name="cross",
-    )(pairs, spread.reshape(DEVICES * 2 * S_BLK, LANES))
+    )(pairs.T, spread.reshape(DEVICES * 2 * S_BLK, LANES))
     owned = lax.all_to_all(
         cross.reshape(DEVICES, 4, LANES), BOTH, split_axis=0, concat_axis=0, tiled=True
     )

time: 100 us -> 99.6 us (level)
  blocking collectives: 0 us -> 90.5 us
  waiting for transfers between devices: 66.2 us -> 0 us
  starting transfers between devices: 21.2 us -> 0 us
  other arithmetic: 2.92 us -> 0 us
    all_to_all x0 -> x2, blocking collectives: none -> 90.5 us  [the longest x1 69.5 us: shards(): lax.all_to_all(whitened.reshape(DEVICES, 2 * S_BLK, LANES), BOTH, split_a...]
    all_to_all x2 -> x0, waiting for transfers between devices: 66.2 us -> none  [the longest x1 53.6 us: shards(): lax.all_to_all(whitened.reshape(DEVICES, 2 * S_BLK, LANES), BOTH, split_a...]
    all_to_all x2 -> x0, starting transfers between devices: 21.2 us -> none  [the longest x1 15.7 us: shards(): lax.all_to_all(whitened.reshape(DEVICES, 2 * S_BLK, LANES), BOTH, split_a...]
    sin x1 -> x0, other arithmetic: 2.05 us -> none  [coarse_tables(): table = jnp.concatenate([jnp.cos(phase), jnp.sin(phase)], axis=1)]
  transfers between devices with their start and end apart: 2 -> 0, of which waited for: 2 -> 0; matrix products, arithmetic and copies ran while one was open for 3% -> 0% of each run, Pallas kernels for 0% -> 0%
where the time goes in v6:
time: 99.6 us; the launch traced here: 99.4 us
  blocking collectives  90.5 us (91%)
  Pallas kernels  8.79 us (9%)
    all_to_all x1, blocking collectives, shards(): lax.all_to_all(whitened.reshape(DEVICES, 2 * S_BLK, LANES), BOTH, split_a...  69.5 us
    all_to_all x1, blocking collectives, shards(): lax.all_to_all(cross.reshape(DEVICES, 4, LANES), BOTH, split_axis=0, conc...  21 us
    pallas_call x1, Pallas kernels, shards(): pl.pallas_call(whiten_kernel, out_shape=jax.ShapeDtypeStruct((DEVICES * 2...  4.11 us
    pallas_call x1, Pallas kernels, shards(): pl.pallas_call(cross_kernel, out_shape=jax.ShapeDtypeStruct((DEVICES * 4,...  3 us

profile of v6, /device:TPU:1, one launch (start us, length us, event | category | flops | bytes accessed | tf_op | source)
XLA Modules:
  0.0 99.4 jit_solution(13452217341538753322)
XLA Ops:
  0.0 4.1 %whiten.1 = bf16[8192,128]{1,0:T(8,128)(2,1)} custom-call(bf16[8192,128]{1,0:T(8,128)(2,1)} %bitcast.17, s32[8,16]{1,0:T(8,128)} %bitcast.18), custom_call_target="tpu_custom_call" | custom-call | tf_op jit(solution)/shard_map/whiten/pallas_call | solution.py:205
  4.1 0.0 copy-start.4
  4.1 69.5 %all_to_all.10 = bf16[256,32,128]{2,1,0:T(8,128)(2,1)S(1)} all-to-all(bf16[256,32,128]{2,1,0:T(8,128)(2,1)} %bitcast.16), channel_id=1, replica_groups=mesh['block'=16,'day'=16] {'block','day'}, dimensions={0} | all-to-all | bytes 4194304 | tf_op jit(solution)/shard_map/all_to_all | solution.py:224
  73.6 0.0 copy-start
  73.6 0.0 copy-start.1
  73.6 0.0 copy-start.2
  73.6 0.0 copy-start.3
  73.6 0.0 copy-done.4
  73.6 3.0 %cross.1 = bf16[1024,128]{1,0:T(8,128)(2,1)S(1)} custom-call(s32[2,16]{1,0:T(2,128)S(1)} %bitcast.15, bf16[8192,128]{1,0:T(8,128)(2,1)S(1)} %bitcast.12), custom_call_target="tpu_custom_call" | custom-call | tf_op jit(solution)/shard_map/cross/pallas_call | solution.py:227
  76.7 21.0 %all_to_all.11 = bf16[256,4,128]{2,1,0:T(4,128)(2,1)S(1)} all-to-all(bf16[256,4,128]{2,1,0:T(4,128)(2,1)S(1)} %bitcast.13), channel_id=1, replica_groups=mesh['block'=16,'day'=16] {'block','day'}, dimensions={0} | all-to-all | bytes 524288 | tf_op jit(solution)/shard_map/all_to_all | solution.py:241
  97.7 0.0 copy-done
  97.7 0.0 copy-done.1
  97.7 0.0 copy-done.2
  97.7 0.0 copy-done.3
  97.7 1.7 %lag.1 = f32[16,2048]{1,0:T(8,128)} custom-call(bf16[1024,128]{1,0:T(8,128)(2,1)S(1)} %bitcast.14, bf16[256,1024]{1,0:T(8,128)(2,1)S(1)} %copy-done.1, bf16[256,1024]{1,0:T(8,128)(2,1)S(1)} %copy-done, f32[64,512]{1,0:T(8,128)S(1)} %copy-done.3, f32[64,512]{1,0:T(8,128)S(1)} %copy-done.2), custom_call_target="tpu_custom_call" | custom-call | tf_op jit(solution)/shard_map/lag/pallas_call | solution.py:246
Async XLA Ops:
  4.1 69.5 %copy-start.4 = (s32[16,2]{0,1:T(2,128)S(1)}, s32[16,2]{0,1:T(2,128)}, u32[]{:S(2)}) copy-start(s32[16,2]{0,1:T(2,128)} %param.9) | copy-start | bytes 388
  73.6 24.1 %copy-start = (bf16[256,1024]{1,0:T(8,128)(2,1)S(1)}, bf16[256,1024]{1,0:T(8,128)(2,1)}, u32[]{:S(2)}) copy-start(bf16[256,1024]{1,0:T(8,128)(2,1)} %constant.9.clone.low_ref) | copy-start | bytes 1572868
  73.6 24.1 %copy-start.1 = (bf16[256,1024]{1,0:T(8,128)(2,1)S(1)}, bf16[256,1024]{1,0:T(8,128)(2,1)}, u32[]{:S(2)}) copy-start(bf16[256,1024]{1,0:T(8,128)(2,1)} %constant.8.clone.high_ref) | copy-start | bytes 1572868
  73.6 24.1 %copy-start.2 = (f32[64,512]{1,0:T(8,128)S(1)}, f32[64,512]{1,0:T(8,128)}, u32[]{:S(2)}) copy-start(f32[64,512]{1,0:T(8,128)} %constant.11.clone.sin_ref) | copy-start | bytes 393220
  73.6 24.1 %copy-start.3 = (f32[64,512]{1,0:T(8,128)S(1)}, f32[64,512]{1,0:T(8,128)}, u32[]{:S(2)}) copy-start(f32[64,512]{1,0:T(8,128)} %constant.10.clone.cos_ref) | copy-start | bytes 393220

commit v7 on v6

--- a/solution.py
+++ b/solution.py
@@ -26,7 +26,7 @@
 QUARTER = DEVICES * 2 * S_BLK // 4
 BOTH = ("block", "day")
 VMEM = pl.BlockSpec(memory_space=pltpu.VMEM)
-ANY = pl.BlockSpec(memory_space=pl.ANY)
+HBM = pl.BlockSpec(memory_space=pltpu.HBM)
 SMEM = pl.BlockSpec(memory_space=pltpu.SMEM)
 
 
@@ -47,24 +47,18 @@
 def whiten_kernel(
     x_hbm,
     mask_hbm,
-    out_hbm,
+    out_ref,
     x_ref,
     mask_ref,
     rows_ref,
     factor_ref,
     valid_ref,
-    out_ref,
     in_sem,
     mask_sem,
-    out_sem,
 ):
     def read(h):
         here = x_hbm.at[pl.ds(h * S_BLK * 64, S_BLK * 64)]
         return pltpu.make_async_copy(here, x_ref.at[h], in_sem.at[h])
-
-    def write(q):
-        here = pl.ds(q * QUARTER, QUARTER)
-        return pltpu.make_async_copy(out_ref.at[here], out_hbm.at[here], out_sem.at[q])
 
     mask_copy = pltpu.make_async_copy(mask_hbm, mask_ref, mask_sem)
     mask_copy.start()
@@ -105,12 +99,9 @@
                 row = (part // 2 * GROUPS + g) * (2 * S_BLK) + part % 2 * S_BLK
                 row = pl.multiple_of(q * QUARTER + row, S_BLK)
                 out_ref[pl.ds(row, S_BLK), :] = mixed[(-g) % GROUPS]
-        write(q).start()
         return carry
 
     lax.fori_loop(0, 4, quarter, 0)
-    for q in range(4):
-        write(q).wait()
 
 
 def cross_kernel(pairs_ref, x_ref, out_ref, whole_ref, keep_ref, place_ref, flat_ref):
@@ -205,20 +196,18 @@
     whitened = pl.pallas_call(
         whiten_kernel,
         out_shape=jax.ShapeDtypeStruct((DEVICES * 2 * S_BLK, LANES), jnp.bfloat16),
-        in_specs=[ANY, ANY],
-        out_specs=ANY,
+        in_specs=[HBM, HBM],
+        out_specs=VMEM,
         scratch_shapes=[
             pltpu.VMEM((HOURS, S_BLK * 64, LANES), jnp.bfloat16),
             pltpu.VMEM((HOURS, S_BLK), jnp.int32),
             pltpu.VMEM((HOURS, S_BLK * PITCH, LANES), jnp.float32),
             pltpu.VMEM((HOURS * S_BLK, LANES), jnp.float32),
             pltpu.VMEM((HOURS * S_BLK, LANES), jnp.float32),
-            pltpu.VMEM((DEVICES * 2 * S_BLK, LANES), jnp.bfloat16),
             pltpu.SemaphoreType.DMA((HOURS,)),
             pltpu.SemaphoreType.DMA,
-            pltpu.SemaphoreType.DMA((4,)),
         ],
-        compiler_params=pltpu.CompilerParams(vmem_limit_bytes=60 * 1024 * 1024),
+        compiler_params=pltpu.CompilerParams(vmem_limit_bytes=50 * 1024 * 1024),
         name="whiten",
     )(values, hour_mask[0])
     spread = lax.all_to_all(

time: 99.6 us -> 98.9 us (level)
  Pallas kernels: 8.79 us -> 7.59 us
    pallas_call x1, Pallas kernels: 4.11 us -> 2.9 us  [shards(): pl.pallas_call(whiten_kernel, out_shape=jax.ShapeDtypeStruct((DEVICES * 2...]
where the time goes in v7:
time: 98.9 us; the launch traced here: 98.7 us
  blocking collectives  90.3 us (91%)
  Pallas kernels  7.59 us (8%)
    all_to_all x1, blocking collectives, shards(): lax.all_to_all(whitened.reshape(DEVICES, 2 * S_BLK, LANES), BOTH, split_a...  69.3 us
    all_to_all x1, blocking collectives, shards(): lax.all_to_all(cross.reshape(DEVICES, 4, LANES), BOTH, split_axis=0, conc...  21 us
    pallas_call x1, Pallas kernels, shards(): pl.pallas_call(cross_kernel, out_shape=jax.ShapeDtypeStruct((DEVICES * 4,...  3 us
    pallas_call x1, Pallas kernels, shards(): pl.pallas_call(whiten_kernel, out_shape=jax.ShapeDtypeStruct((DEVICES * 2...  2.9 us

profile of v7, /device:TPU:1, one launch (start us, length us, event | category | flops | bytes accessed | tf_op | source)
XLA Modules:
  0.0 98.7 jit_solution(4425679580942783534)
XLA Ops:
  0.0 0.0 copy-start.4
  0.0 0.7 copy-done.4
  0.7 2.9 %whiten.1 = bf16[8192,128]{1,0:T(8,128)(2,1)S(1)} custom-call(bf16[8192,128]{1,0:T(8,128)(2,1)} %bitcast.18, s32[8,16]{1,0:T(8,128)S(1)} %bitcast.16), custom_call_target="tpu_custom_call" | custom-call | tf_op jit(solution)/shard_map/whiten/pallas_call | solution.py:196
  3.6 0.0 copy-start.5
  3.6 69.3 %all_to_all.10 = bf16[256,32,128]{2,1,0:T(8,128)(2,1)S(1)} all-to-all(bf16[256,32,128]{2,1,0:T(8,128)(2,1)S(1)} %bitcast.12), channel_id=1, replica_groups=mesh['block'=16,'day'=16] {'block','day'}, dimensions={0} | all-to-all | bytes 4194304 | tf_op jit(solution)/shard_map/all_to_all | solution.py:213
  72.9 0.0 copy-start
  72.9 0.0 copy-start.1
  72.9 0.0 copy-start.2
  72.9 0.0 copy-start.3
  72.9 0.0 copy-done.5
  72.9 3.0 %cross.1 = bf16[1024,128]{1,0:T(8,128)(2,1)S(1)} custom-call(s32[2,16]{1,0:T(2,128)S(1)} %bitcast.17, bf16[8192,128]{1,0:T(8,128)(2,1)S(1)} %bitcast.13), custom_call_target="tpu_custom_call" | custom-call | tf_op jit(solution)/shard_map/cross/pallas_call | solution.py:216
  75.9 21.0 %all_to_all.11 = bf16[256,4,128]{2,1,0:T(4,128)(2,1)S(1)} all-to-all(bf16[256,4,128]{2,1,0:T(4,128)(2,1)S(1)} %bitcast.14), channel_id=1, replica_groups=mesh['block'=16,'day'=16] {'block','day'}, dimensions={0} | all-to-all | bytes 524288 | tf_op jit(solution)/shard_map/all_to_all | solution.py:230
  97.0 0.0 copy-done
  97.0 0.0 copy-done.1
  97.0 0.0 copy-done.2
  97.0 0.0 copy-done.3
  97.0 1.7 %lag.1 = f32[16,2048]{1,0:T(8,128)} custom-call(bf16[1024,128]{1,0:T(8,128)(2,1)S(1)} %bitcast.15, bf16[256,1024]{1,0:T(8,128)(2,1)S(1)} %copy-done.1, bf16[256,1024]{1,0:T(8,128)(2,1)S(1)} %copy-done, f32[64,512]{1,0:T(8,128)S(1)} %copy-done.3, f32[64,512]{1,0:T(8,128)S(1)} %copy-done.2), custom_call_target="tpu_custom_call" | custom-call | tf_op jit(solution)/shard_map/lag/pallas_call | solution.py:235
Async XLA Ops:
  0.0 0.7 copy-start.4
  3.6 69.3 %copy-start.5 = (s32[16,2]{0,1:T(2,128)S(1)}, s32[16,2]{0,1:T(2,128)}, u32[]{:S(2)}) copy-start(s32[16,2]{0,1:T(2,128)} %param.9) | copy-start | bytes 388
  72.9 24.1 %copy-start = (bf16[256,1024]{1,0:T(8,128)(2,1)S(1)}, bf16[256,1024]{1,0:T(8,128)(2,1)}, u32[]{:S(2)}) copy-start(bf16[256,1024]{1,0:T(8,128)(2,1)} %constant.9.clone.low_ref) | copy-start | bytes 1572868
  72.9 24.1 %copy-start.1 = (bf16[256,1024]{1,0:T(8,128)(2,1)S(1)}, bf16[256,1024]{1,0:T(8,128)(2,1)}, u32[]{:S(2)}) copy-start(bf16[256,1024]{1,0:T(8,128)(2,1)} %constant.8.clone.high_ref) | copy-start | bytes 1572868
  72.9 24.1 %copy-start.2 = (f32[64,512]{1,0:T(8,128)S(1)}, f32[64,512]{1,0:T(8,128)}, u32[]{:S(2)}) copy-start(f32[64,512]{1,0:T(8,128)} %constant.11.clone.sin_ref) | copy-start | bytes 393220
  72.9 24.1 %copy-start.3 = (f32[64,512]{1,0:T(8,128)S(1)}, f32[64,512]{1,0:T(8,128)}, u32[]{:S(2)}) copy-start(f32[64,512]{1,0:T(8,128)} %constant.10.clone.cos_ref) | copy-start | bytes 393220

commit v8 on v7

--- a/solution.py
+++ b/solution.py
@@ -101,7 +101,8 @@
                 out_ref[pl.ds(row, S_BLK), :] = mixed[(-g) % GROUPS]
         return carry
 
-    lax.fori_loop(0, 4, quarter, 0)
+    for q in range(4):
+        quarter(q, 0)
 
 
 def cross_kernel(pairs_ref, x_ref, out_ref, whole_ref, keep_ref, place_ref, flat_ref):

time: 98.9 us -> 98.7 us (level)
  no operation moved by 1% of the time
where the time goes in v8:
time: 98.7 us; the launch traced here: 98.6 us
  blocking collectives  90.3 us (91%)
  Pallas kernels  7.47 us (8%)
    all_to_all x1, blocking collectives, shards(): lax.all_to_all(whitened.reshape(DEVICES, 2 * S_BLK, LANES), BOTH, split_a...  69.3 us
    all_to_all x1, blocking collectives, shards(): lax.all_to_all(cross.reshape(DEVICES, 4, LANES), BOTH, split_axis=0, conc...  21 us
    pallas_call x1, Pallas kernels, shards(): pl.pallas_call(cross_kernel, out_shape=jax.ShapeDtypeStruct((DEVICES * 4,...  3.01 us
    pallas_call x1, Pallas kernels, shards(): pl.pallas_call(whiten_kernel, out_shape=jax.ShapeDtypeStruct((DEVICES * 2...  2.76 us

profile of v8, /device:TPU:1, one launch (start us, length us, event | category | flops | bytes accessed | tf_op | source)
XLA Modules:
  0.0 98.6 jit_solution(9250819108863485130)
XLA Ops:
  0.0 0.0 copy-start.4
  0.0 0.7 copy-done.4
  0.7 2.8 %whiten.1 = bf16[8192,128]{1,0:T(8,128)(2,1)S(1)} custom-call(bf16[8192,128]{1,0:T(8,128)(2,1)} %bitcast.18, s32[8,16]{1,0:T(8,128)S(1)} %bitcast.16), custom_call_target="tpu_custom_call" | custom-call | tf_op jit(solution)/shard_map/whiten/pallas_call | solution.py:197
  3.5 0.0 copy-start.5
  3.5 69.3 %all_to_all.10 = bf16[256,32,128]{2,1,0:T(8,128)(2,1)S(1)} all-to-all(bf16[256,32,128]{2,1,0:T(8,128)(2,1)S(1)} %bitcast.12), channel_id=1, replica_groups=mesh['block'=16,'day'=16] {'block','day'}, dimensions={0} | all-to-all | bytes 4194304 | tf_op jit(solution)/shard_map/all_to_all | solution.py:214
  72.8 0.0 copy-start
  72.8 0.0 copy-start.1
  72.8 0.0 copy-start.2
  72.8 0.0 copy-start.3
  72.8 0.0 copy-done.5
  72.8 3.0 %cross.1 = bf16[1024,128]{1,0:T(8,128)(2,1)S(1)} custom-call(s32[2,16]{1,0:T(2,128)S(1)} %bitcast.17, bf16[8192,128]{1,0:T(8,128)(2,1)S(1)} %bitcast.13), custom_call_target="tpu_custom_call" | custom-call | tf_op jit(solution)/shard_map/cross/pallas_call | solution.py:217
  75.8 21.0 %all_to_all.11 = bf16[256,4,128]{2,1,0:T(4,128)(2,1)S(1)} all-to-all(bf16[256,4,128]{2,1,0:T(4,128)(2,1)S(1)} %bitcast.14), channel_id=1, replica_groups=mesh['block'=16,'day'=16] {'block','day'}, dimensions={0} | all-to-all | bytes 524288 | tf_op jit(solution)/shard_map/all_to_all | solution.py:231
  96.8 0.0 copy-done
  96.8 0.0 copy-done.1
  96.8 0.0 copy-done.2
  96.9 0.0 copy-done.3
  96.9 1.7 %lag.1 = f32[16,2048]{1,0:T(8,128)} custom-call(bf16[1024,128]{1,0:T(8,128)(2,1)S(1)} %bitcast.15, bf16[256,1024]{1,0:T(8,128)(2,1)S(1)} %copy-done.1, bf16[256,1024]{1,0:T(8,128)(2,1)S(1)} %copy-done, f32[64,512]{1,0:T(8,128)S(1)} %copy-done.3, f32[64,512]{1,0:T(8,128)S(1)} %copy-done.2), custom_call_target="tpu_custom_call" | custom-call | tf_op jit(solution)/shard_map/lag/pallas_call | solution.py:236
Async XLA Ops:
  0.0 0.7 copy-start.4
  3.5 69.3 %copy-start.5 = (s32[16,2]{0,1:T(2,128)S(1)}, s32[16,2]{0,1:T(2,128)}, u32[]{:S(2)}) copy-start(s32[16,2]{0,1:T(2,128)} %param.9) | copy-start | bytes 388
  72.8 24.1 %copy-start = (bf16[256,1024]{1,0:T(8,128)(2,1)S(1)}, bf16[256,1024]{1,0:T(8,128)(2,1)}, u32[]{:S(2)}) copy-start(bf16[256,1024]{1,0:T(8,128)(2,1)} %constant.9.clone.low_ref) | copy-start | bytes 1572868
  72.8 24.1 %copy-start.1 = (bf16[256,1024]{1,0:T(8,128)(2,1)S(1)}, bf16[256,1024]{1,0:T(8,128)(2,1)}, u32[]{:S(2)}) copy-start(bf16[256,1024]{1,0:T(8,128)(2,1)} %constant.8.clone.high_ref) | copy-start | bytes 1572868
  72.8 24.1 %copy-start.2 = (f32[64,512]{1,0:T(8,128)S(1)}, f32[64,512]{1,0:T(8,128)}, u32[]{:S(2)}) copy-start(f32[64,512]{1,0:T(8,128)} %constant.11.clone.sin_ref) | copy-start | bytes 393220
  72.8 24.1 %copy-start.3 = (f32[64,512]{1,0:T(8,128)S(1)}, f32[64,512]{1,0:T(8,128)}, u32[]{:S(2)}) copy-start(f32[64,512]{1,0:T(8,128)} %constant.10.clone.cos_ref) | copy-start | bytes 393220
